TPU v7x, 512 devices: a whole 4x8x8 slice. The times are simulated.
512 devices in a mesh: snap: 8 (over x, core), space: 64 (over z, y).
Axes of the slice: x: 4, y: 8, z: 8, core: 2. Of those that a mesh axis runs over, the one named last changes fastest.
Arguments:
- velocity: float32 [2, 64, 2048, 1024], P(None, 'snap', 'space'), may hold values from -820 to 820
- metric_index: int32 [2048, 1024], P('space'), may hold values from 0 to 15
- metric_table: float32 [4, 16], replicated, may hold values from -2 to 2
Outputs:
- mode_field: float32 [63, 2048, 1024], P(None, 'space', 'snap')
- operator: float32 [63, 63], replicated
All inputs are finite; a program needn't handle non-finite values.
Results may differ from a plain program's by a relative error of at most 0.00027.
Values sent between devices are 32-bit elements; how exact they have to be, the bound alone decides.
No kernel may reach another device: no remote copies, remote signals or barrier semaphores. Data moves between devices by JAX's collectives and lax.ppermute only.
A program may use at most 64 MiB of HBM per device.

v0:
```python
import jax
import jax.numpy as jnp
from jax import lax
from jax.sharding import PartitionSpec as P


def extended(array, sides, width):
    for axis, dim in sides:
        size, length = (lax.axis_size(axis), array.shape[dim])
        up = [(i, (i + 1) % size) for i in range(size - 1)]
        down = [(j, i) for i, j in up]
        last = lax.slice_in_dim(array, length - width, length, axis=dim)
        first = lax.slice_in_dim(array, 0, width, axis=dim)
        before = lax.ppermute(last, axis, up)
        after = lax.ppermute(first, axis, down)
        array = jnp.concatenate([before, array, after], axis=dim)
    return array


def partner_2(value, axis, apart):
    mask = 2**apart
    pairs = [(source, source ^ mask) for source in range(lax.axis_size(axis))]
    return lax.ppermute(value, axis, pairs)


def along_rows(padded, row_count):
    near_diff = padded[:, :, 4 : 4 + row_count, :] - padded[:, :, 2 : 2 + row_count, :]
    middle = padded[:, :, 5 : 5 + row_count, :] - padded[:, :, 1 : 1 + row_count, :]
    far_diff = padded[:, :, 6 : 6 + row_count, :] - padded[:, :, 0:row_count, :]
    return (45.0 * near_diff - 9.0 * middle + far_diff) / 60.0


def along_cycle(field):
    near_diff = jnp.roll(field, -1, axis=-1) - jnp.roll(field, 1, axis=-1)
    middle = jnp.roll(field, -2, axis=-1) - jnp.roll(field, 2, axis=-1)
    far_diff = jnp.roll(field, -3, axis=-1) - jnp.roll(field, 3, axis=-1)
    return (45.0 * near_diff - 9.0 * middle + far_diff) / 60.0


def metric_lookup(metric_table, metric_index):
    classes = metric_table.shape[1]
    onehot = (
        metric_index[None, :, :] == jnp.arange(classes, dtype=jnp.int32)[:, None, None]
    ).astype(jnp.float32)
    return jnp.einsum("ck,kxy->cxy", metric_table, onehot, precision=lax.Precision.HIGHEST)


def vorticity_of(velocity, padded, metric):
    row_count = velocity.shape[2]
    row_derivs = along_rows(padded, row_count)
    cycle_derivs = along_cycle(velocity)
    return (
        metric[0] * row_derivs[1]
        + metric[1] * cycle_derivs[1]
        - metric[2] * row_derivs[0]
        - metric[3] * cycle_derivs[0]
    )


def upper_factor(matrix):
    return jnp.linalg.cholesky(matrix).T


def lower_solve(lower_mat, right_rows):
    return jax.scipy.linalg.solve_triangular(lower_mat, right_rows, lower=True)


def local(velocity, metric_index, metric_table):
    padded = extended(velocity, (("space", 2),), 3)
    metric = metric_lookup(metric_table, metric_index)
    vorticity = vorticity_of(velocity, padded, metric)
    regrouped = lax.all_to_all(vorticity, "snap", split_axis=2, concat_axis=0, tiled=True)
    snap_count = regrouped.shape[0]
    snapshot_rows = regrouped.reshape(snap_count, regrouped.shape[1] * regrouped.shape[2])
    device_count = lax.axis_size("snap") * lax.axis_size("space")
    inverse_count = 1.0 / (snapshot_rows.shape[1] * device_count)
    local_gram = (
        jnp.dot(snapshot_rows, snapshot_rows.T, precision=lax.Precision.HIGHEST) * inverse_count
    )
    running = local_gram
    levels = device_count.bit_length() - 1
    for level_bit in range(levels):
        partner = partner_2(running, ("snap", "space"), level_bit)
        running = running + partner
    factor = upper_factor(running)
    order_less = snap_count - 1
    leading = factor[:order_less, :order_less]
    coupling = factor[:order_less, 1:]
    shifted = snapshot_rows[1:]
    operator = lower_solve(leading.T, coupling.T).T
    mode_rows = lower_solve(leading.T, shifted)
    return (mode_rows.reshape(order_less, regrouped.shape[1], regrouped.shape[2]), operator)


def solution(mesh):
    in_specs = (P(None, "snap", "space", None), P("space", None), P())
    out_specs = (P(None, "space", "snap"), P())
    return jax.shard_map(local, mesh=mesh, in_specs=in_specs, out_specs=out_specs, check_vma=False)
```

profile of v0, /device:TPU:56, one launch (start us, length us, event | category | flops | bytes accessed | tf_op | source)
XLA Modules:
  0.0 141.7 jit_solution(18227473084230369310)
XLA Ops:
  2.1 3.3 %collective-permute-start = (f32[2,8,3,1024]{3,1,2,0:T(8,128)S(1)}, f32[2,8,3,1024]{3,1,2,0:T(8,128)S(1)}, u32[]{:S(2)}, u32[]{:S(2)}) collective-permute-start(f32[2,8,3,1024]{3,1,2,0:T(8,128)S(1)} %copy.107), channel_id=1, source_target_pairs={{1,0},{2,1},{3,2},{4,3},{5,4},{6,5},{7,6},{8,7},{9,8},{10,9},{11,1... | collective-permute-start | bytes 589832 | tf_op jit(solution)/shard_map/ppermute | solution.py:15
  5.5 4.8 %collective-permute-start.1 = (f32[2,8,3,1024]{3,1,2,0:T(8,128)S(1)}, f32[2,8,3,1024]{3,1,2,0:T(8,128)S(1)}, u32[]{:S(2)}, u32[]{:S(2)}) collective-permute-start(f32[2,8,3,1024]{3,1,2,0:T(8,128)S(1)} %copy.108), channel_id=1, source_target_pairs={{0,1},{1,2},{2,3},{3,4},{4,5},{5,6},{6,7},{7,8},{8,9},{9,10},{10,1... | collective-permute-start | bytes 589832 | tf_op jit(solution)/shard_map/ppermute | solution.py:14
  10.3 3.1 %fusion.37 = (f32[2,8,32,1021]{3,2,1,0:T(8,128)S(1)}, f32[2,8,32,1021]{3,2,1,0:T(8,128)S(1)}) fusion(f32[2,8,32,1024]{3,2,1,0:T(8,128)} %param.3), kind=kLoop, calls=%fused_computation.67 | loop fusion | bytes 8364032 | tf_op jit(solution)/shard_map/jit(_roll_static)/slice | solution.py:36
  17.2 3.1 %fusion.13 = f32[2,8,32,1024]{3,2,1,0:T(8,128)S(1)} fusion(f32[2,8,32,1]{3,2,1,0:T(8,128)S(1)} %get-tuple-element.25, f32[2,8,32,1023]{3,2,1,0:T(8,128)S(1)} %get-tuple-element.27, f32[2,8,32,1023]{3,2,1,0:T(8,128)S(1)} %get-tuple-element.26, f32[2,8,32,1]{3,2,1,0:T(8,128)S(1)} %get-tuple-element.24, f32[2,8,32,2]{3,2,1,0:T(8,128)S(1)} %get-tuple-element.21, ...), kind=kLoop, calls=%fused_computation.19 | loop fusion | flops 7340032 | bytes 14680064 | tf_op jit(solution)/shard_map/div | solution.py:37
  23.0 2.7 %copy.93 = f32[8,32,1024]{1,0,2:T(8,128)} copy(f32[8,32,1024]{2,1,0:T(8,128)S(1)} %fusion.18) | data formatting | bytes 2097152 | tf_op jit(solution)/shard_map/sub | solution.py:53
  25.7 3.9 %reshape.27 = f32[8,1,32768]{2,1,0:T(1,128)S(1)} reshape(f32[1024,8,32]{2,1,0:T(8,128)} %bitcast.79) | data formatting | bytes 2097152
  29.6 20.2 %all_to_all.15 = f32[8,1,32768]{2,1,0:T(1,128)S(1)} all-to-all(f32[8,1,32768]{2,1,0:T(1,128)S(1)} %reshape.27), channel_id=1, replica_groups=mesh['snap'=8,'space'=64] {'snap'}, dimensions={0} | all-to-all | bytes 2097152 | tf_op jit(solution)/shard_map/all_to_all | solution.py:72
  50.3 3.2 %reduce.6 = f32[8,32768]{1,0:T(8,128)S(1)} reduce(f32[8,1,32768]{2,1,0:T(1,128)S(1)} %all_to_all.15, f32[]{:T(128)} %broadcast.92), dimensions={1}, to_apply=%all_to_all.11.reduce_sub_computation | reduce | bytes 2097156 | tf_op jit(solution)/shard_map/all_to_all | solution.py:72
  53.6 3.3 %reshape.28 = f32[1024,8,32]{2,1,0:T(8,128)} reshape(f32[8,32768]{1,0:T(8,128)S(1)} %reduce.6) | data formatting | bytes 2097152
  56.9 2.8 %copy.94 = f32[8,32,8,128]{3,1,0,2:T(8,128)S(1)} copy(f32[8,32,8,128]{1,0,3,2:T(8,128)} %bitcast.80) | data formatting | bytes 2097152 | tf_op jit(solution)/shard_map/all_to_all | solution.py:72
  59.7 2.0 %convolution_multiply_fusion = f32[64,64]{0,1:T(8,128)S(1)} fusion(f32[8,8,32,128]{3,2,1,0:T(8,128)S(1)} %bitcast.81), kind=kOutput, calls=%fused_computation.26 | convolution fusion | flops 201330688 | bytes 1064960 | tf_op jit(solution)/shard_map/dot_general | solution.py:78
  61.7 1.9 %collective-permute-start.2 = (f32[64,64]{0,1:T(8,128)S(1)}, f32[64,64]{0,1:T(8,128)S(1)}, u32[]{:S(2)}, u32[]{:S(2)}) collective-permute-start(f32[64,64]{0,1:T(8,128)S(1)} %convolution_multiply_fusion), channel_id=1, source_target_pairs={{0,1},{1,0},{2,3},{3,2},{4,5},{5,4},{6,7},{7,6},{8,9},{9,8},{10,11... | collective-permute-start | bytes 49160 | tf_op jit(solution)/shard_map/ppermute | solution.py:23
  63.7 3.9 %collective-permute-done.2 = f32[64,64]{0,1:T(8,128)S(1)} collective-permute-done((f32[64,64]{0,1:T(8,128)S(1)}, f32[64,64]{0,1:T(8,128)S(1)}, u32[]{:S(2)}, u32[]{:S(2)}) %collective-permute-start.2) | collective-permute-done | bytes 16416 | tf_op jit(solution)/shard_map/ppermute | solution.py:23
  67.6 1.9 %collective-permute-start.3 = (f32[64,64]{0,1:T(8,128)S(1)}, f32[64,64]{0,1:T(8,128)S(1)}, u32[]{:S(2)}, u32[]{:S(2)}) collective-permute-start(f32[64,64]{0,1:T(8,128)S(1)} %add.54), channel_id=1, source_target_pairs={{0,2},{1,3},{2,0},{3,1},{4,6},{5,7},{6,4},{7,5},{8,10},{9,11},{10,... | collective-permute-start | bytes 49160 | tf_op jit(solution)/shard_map/ppermute | solution.py:23
  69.5 4.8 %collective-permute-done.3 = f32[64,64]{0,1:T(8,128)S(1)} collective-permute-done((f32[64,64]{0,1:T(8,128)S(1)}, f32[64,64]{0,1:T(8,128)S(1)}, u32[]{:S(2)}, u32[]{:S(2)}) %collective-permute-start.3) | collective-permute-done | bytes 16416 | tf_op jit(solution)/shard_map/ppermute | solution.py:23
  74.3 4.0 %collective-permute-start.4 = (f32[64,64]{0,1:T(8,128)S(1)}, f32[64,64]{0,1:T(8,128)S(1)}, u32[]{:S(2)}, u32[]{:S(2)}) collective-permute-start(f32[64,64]{0,1:T(8,128)S(1)} %add.55), channel_id=1, source_target_pairs={{0,4},{1,5},{2,6},{3,7},{4,0},{5,1},{6,2},{7,3},{8,12},{9,13},{10,... | collective-permute-start | bytes 49160 | tf_op jit(solution)/shard_map/ppermute | solution.py:23
  78.2 6.1 %collective-permute-done.4 = f32[64,64]{0,1:T(8,128)S(1)} collective-permute-done((f32[64,64]{0,1:T(8,128)S(1)}, f32[64,64]{0,1:T(8,128)S(1)}, u32[]{:S(2)}, u32[]{:S(2)}) %collective-permute-start.4) | collective-permute-done | bytes 16416 | tf_op jit(solution)/shard_map/ppermute | solution.py:23
  84.3 3.9 %collective-permute-start.5 = (f32[64,64]{0,1:T(8,128)S(1)}, f32[64,64]{0,1:T(8,128)S(1)}, u32[]{:S(2)}, u32[]{:S(2)}) collective-permute-start(f32[64,64]{0,1:T(8,128)S(1)} %add.56), channel_id=1, source_target_pairs={{0,8},{1,9},{2,10},{3,11},{4,12},{5,13},{6,14},{7,15},{8,0},{9,1},... | collective-permute-start | bytes 49160 | tf_op jit(solution)/shard_map/ppermute | solution.py:23
  88.3 1.9 %collective-permute-done.5 = f32[64,64]{0,1:T(8,128)S(1)} collective-permute-done((f32[64,64]{0,1:T(8,128)S(1)}, f32[64,64]{0,1:T(8,128)S(1)}, u32[]{:S(2)}, u32[]{:S(2)}) %collective-permute-start.5) | collective-permute-done | bytes 16416 | tf_op jit(solution)/shard_map/ppermute | solution.py:23
  90.1 7.6 %collective-permute-start.6 = (f32[64,64]{0,1:T(8,128)S(1)}, f32[64,64]{0,1:T(8,128)S(1)}, u32[]{:S(2)}, u32[]{:S(2)}) collective-permute-start(f32[64,64]{0,1:T(8,128)S(1)} %add.57), channel_id=1, source_target_pairs={{0,16},{1,17},{2,18},{3,19},{4,20},{5,21},{6,22},{7,23},{8,24},{9,... | collective-permute-start | bytes 49160 | tf_op jit(solution)/shard_map/ppermute | solution.py:23
  97.7 1.9 %collective-permute-done.6 = f32[64,64]{0,1:T(8,128)S(1)} collective-permute-done((f32[64,64]{0,1:T(8,128)S(1)}, f32[64,64]{0,1:T(8,128)S(1)}, u32[]{:S(2)}, u32[]{:S(2)}) %collective-permute-start.6) | collective-permute-done | bytes 16416 | tf_op jit(solution)/shard_map/ppermute | solution.py:23
  99.6 7.8 %collective-permute-start.7 = (f32[64,64]{0,1:T(8,128)S(1)}, f32[64,64]{0,1:T(8,128)S(1)}, u32[]{:S(2)}, u32[]{:S(2)}) collective-permute-start(f32[64,64]{0,1:T(8,128)S(1)} %add.58), channel_id=1, source_target_pairs={{0,32},{1,33},{2,34},{3,35},{4,36},{5,37},{6,38},{7,39},{8,40},{9,... | collective-permute-start | bytes 49160 | tf_op jit(solution)/shard_map/ppermute | solution.py:23
  107.4 1.9 %collective-permute-done.7 = f32[64,64]{0,1:T(8,128)S(1)} collective-permute-done((f32[64,64]{0,1:T(8,128)S(1)}, f32[64,64]{0,1:T(8,128)S(1)}, u32[]{:S(2)}, u32[]{:S(2)}) %collective-permute-start.7) | collective-permute-done | bytes 16416 | tf_op jit(solution)/shard_map/ppermute | solution.py:23
  109.3 1.9 %collective-permute-start.8 = (f32[64,64]{0,1:T(8,128)S(1)}, f32[64,64]{0,1:T(8,128)S(1)}, u32[]{:S(2)}, u32[]{:S(2)}) collective-permute-start(f32[64,64]{0,1:T(8,128)S(1)} %add.59), channel_id=1, source_target_pairs={{0,64},{1,65},{2,66},{3,67},{4,68},{5,69},{6,70},{7,71},{8,72},{9,... | collective-permute-start | bytes 49160 | tf_op jit(solution)/shard_map/ppermute | solution.py:23
  112.4 2.5 %collective-permute-start.9 = (f32[64,64]{0,1:T(8,128)S(1)}, f32[64,64]{0,1:T(8,128)S(1)}, u32[]{:S(2)}, u32[]{:S(2)}) collective-permute-start(f32[64,64]{0,1:T(8,128)S(1)} %add.60), channel_id=1, source_target_pairs={{0,128},{1,129},{2,130},{3,131},{4,132},{5,133},{6,134},{7,135},{8... | collective-permute-start | bytes 49160 | tf_op jit(solution)/shard_map/ppermute | solution.py:23
  115.8 2.4 %collective-permute-done.9 = f32[64,64]{0,1:T(8,128)S(1)} collective-permute-done((f32[64,64]{0,1:T(8,128)S(1)}, f32[64,64]{0,1:T(8,128)S(1)}, u32[]{:S(2)}, u32[]{:S(2)}) %collective-permute-start.9) | collective-permute-done | bytes 16416 | tf_op jit(solution)/shard_map/ppermute | solution.py:23
  118.2 2.7 %collective-permute-start.10 = (f32[64,64]{0,1:T(8,128)S(1)}, f32[64,64]{0,1:T(8,128)S(1)}, u32[]{:S(2)}, u32[]{:S(2)}) collective-permute-start(f32[64,64]{0,1:T(8,128)S(1)} %add.61), channel_id=1, source_target_pairs={{0,256},{1,257},{2,258},{3,259},{4,260},{5,261},{6,262},{7,263},{8... | collective-permute-start | bytes 49160 | tf_op jit(solution)/shard_map/ppermute | solution.py:23
  121.0 4.5 %collective-permute-done.10 = f32[64,64]{0,1:T(8,128)S(1)} collective-permute-done((f32[64,64]{0,1:T(8,128)S(1)}, f32[64,64]{0,1:T(8,128)S(1)}, u32[]{:S(2)}, u32[]{:S(2)}) %collective-permute-start.10) | collective-permute-done | bytes 16416 | tf_op jit(solution)/shard_map/ppermute | solution.py:23
  125.6 5.8 %cholesky.18 = f32[64,64]{1,0:T(8,128)S(1)} custom-call(f32[64,64]{1,0:T(8,128)S(1)} %fusion.33), custom_call_target="Cholesky" | custom-call | tf_op jit(solution)/shard_map/jit(cholesky)/cholesky | solution.py:61
  132.8 4.8 %custom-call.10 = f32[1,63,63]{1,2,0:T(8,128)S(1)} custom-call(f32[1,63,63]{2,1,0:T(8,128)S(1)} %fusion.30), custom_call_target="InvertDiagBlocksLowerTriangular" | custom-call | tf_op jit(solution)/shard_map/jit(_solve_triangular)/triangular_solve | solution.py:65
  138.5 1.6 %fusion.24 = f32[63,32,128]{2,0,1:T(8,128)S(1)} fusion(f32[32,128,63]{1,0,2:T(8,128)S(1)} %slice_bitcast_fusion.4, f32[1,63,63]{1,2,0:T(8,128)S(1)} %custom-call.10), kind=kOutput, calls=%fused_computation.39 | convolution fusion | flops 195084288 | bytes 2080260 | tf_op jit(solution)/shard_map/jit(_solve_triangular)/triangular_solve | solution.py:65
  140.1 1.6 %copy.99 = f32[63,32,128]{2,1,0:T(8,128)} copy(f32[63,32,128]{2,0,1:T(8,128)S(1)} %fusion.24) | data formatting | bytes 2064384
  (47 shorter events, 12.9 us)
Async XLA Ops:
  0.6 14.9 %copy-start = (f32[4,16]{1,0:T(4,128)S(1)}, f32[4,16]{1,0:T(4,128)}, u32[]{:S(2)}) copy-start(f32[4,16]{1,0:T(4,128)} %param.5) | copy-start | bytes 772
  2.1 18.6 %collective-permute-start = (f32[2,8,3,1024]{3,1,2,0:T(8,128)S(1)}, f32[2,8,3,1024]{3,1,2,0:T(8,128)S(1)}, u32[]{:S(2)}, u32[]{:S(2)}) collective-permute-start(f32[2,8,3,1024]{3,1,2,0:T(8,128)S(1)} %copy.107), channel_id=1, source_target_pairs={{1,0},{2,1},{3,2},{4,3},{5,4},{6,5},{7,6},{8,7},{9,8},{10,9},{11,1... | collective-permute-start | bytes 589832 | tf_op jit(solution)/shard_map/ppermute | solution.py:15
  5.5 7.9 %copy-start.1 = (f32[2,8,32,1024]{3,2,1,0:T(8,128)S(1)}, f32[2,8,32,1024]{3,2,1,0:T(8,128)}, u32[]{:S(2)}) copy-start(f32[2,8,32,1024]{3,2,1,0:T(8,128)} %param.3) | copy-start | bytes 6291460
  5.5 15.1 %collective-permute-start.1 = (f32[2,8,3,1024]{3,1,2,0:T(8,128)S(1)}, f32[2,8,3,1024]{3,1,2,0:T(8,128)S(1)}, u32[]{:S(2)}, u32[]{:S(2)}) collective-permute-start(f32[2,8,3,1024]{3,1,2,0:T(8,128)S(1)} %copy.108), channel_id=1, source_target_pairs={{0,1},{1,2},{2,3},{3,4},{4,5},{5,6},{6,7},{7,8},{8,9},{9,10},{10,1... | collective-permute-start | bytes 589832 | tf_op jit(solution)/shard_map/ppermute | solution.py:14
  15.1 0.9 copy-start.2
  61.7 5.8 %collective-permute-start.2 = (f32[64,64]{0,1:T(8,128)S(1)}, f32[64,64]{0,1:T(8,128)S(1)}, u32[]{:S(2)}, u32[]{:S(2)}) collective-permute-start(f32[64,64]{0,1:T(8,128)S(1)} %convolution_multiply_fusion), channel_id=1, source_target_pairs={{0,1},{1,0},{2,3},{3,2},{4,5},{5,4},{6,7},{7,6},{8,9},{9,8},{10,11... | collective-permute-start | bytes 49160 | tf_op jit(solution)/shard_map/ppermute | solution.py:23
  67.6 6.7 %collective-permute-start.3 = (f32[64,64]{0,1:T(8,128)S(1)}, f32[64,64]{0,1:T(8,128)S(1)}, u32[]{:S(2)}, u32[]{:S(2)}) collective-permute-start(f32[64,64]{0,1:T(8,128)S(1)} %add.54), channel_id=1, source_target_pairs={{0,2},{1,3},{2,0},{3,1},{4,6},{5,7},{6,4},{7,5},{8,10},{9,11},{10,... | collective-permute-start | bytes 49160 | tf_op jit(solution)/shard_map/ppermute | solution.py:23
  74.3 10.1 %collective-permute-start.4 = (f32[64,64]{0,1:T(8,128)S(1)}, f32[64,64]{0,1:T(8,128)S(1)}, u32[]{:S(2)}, u32[]{:S(2)}) collective-permute-start(f32[64,64]{0,1:T(8,128)S(1)} %add.55), channel_id=1, source_target_pairs={{0,4},{1,5},{2,6},{3,7},{4,0},{5,1},{6,2},{7,3},{8,12},{9,13},{10,... | collective-permute-start | bytes 49160 | tf_op jit(solution)/shard_map/ppermute | solution.py:23
  84.3 5.8 %collective-permute-start.5 = (f32[64,64]{0,1:T(8,128)S(1)}, f32[64,64]{0,1:T(8,128)S(1)}, u32[]{:S(2)}, u32[]{:S(2)}) collective-permute-start(f32[64,64]{0,1:T(8,128)S(1)} %add.56), channel_id=1, source_target_pairs={{0,8},{1,9},{2,10},{3,11},{4,12},{5,13},{6,14},{7,15},{8,0},{9,1},... | collective-permute-start | bytes 49160 | tf_op jit(solution)/shard_map/ppermute | solution.py:23
  90.1 9.5 %collective-permute-start.6 = (f32[64,64]{0,1:T(8,128)S(1)}, f32[64,64]{0,1:T(8,128)S(1)}, u32[]{:S(2)}, u32[]{:S(2)}) collective-permute-start(f32[64,64]{0,1:T(8,128)S(1)} %add.57), channel_id=1, source_target_pairs={{0,16},{1,17},{2,18},{3,19},{4,20},{5,21},{6,22},{7,23},{8,24},{9,... | collective-permute-start | bytes 49160 | tf_op jit(solution)/shard_map/ppermute | solution.py:23
  99.6 9.7 %collective-permute-start.7 = (f32[64,64]{0,1:T(8,128)S(1)}, f32[64,64]{0,1:T(8,128)S(1)}, u32[]{:S(2)}, u32[]{:S(2)}) collective-permute-start(f32[64,64]{0,1:T(8,128)S(1)} %add.58), channel_id=1, source_target_pairs={{0,32},{1,33},{2,34},{3,35},{4,36},{5,37},{6,38},{7,39},{8,40},{9,... | collective-permute-start | bytes 49160 | tf_op jit(solution)/shard_map/ppermute | solution.py:23
  109.3 3.1 %collective-permute-start.8 = (f32[64,64]{0,1:T(8,128)S(1)}, f32[64,64]{0,1:T(8,128)S(1)}, u32[]{:S(2)}, u32[]{:S(2)}) collective-permute-start(f32[64,64]{0,1:T(8,128)S(1)} %add.59), channel_id=1, source_target_pairs={{0,64},{1,65},{2,66},{3,67},{4,68},{5,69},{6,70},{7,71},{8,72},{9,... | collective-permute-start | bytes 49160 | tf_op jit(solution)/shard_map/ppermute | solution.py:23
  112.4 5.8 %collective-permute-start.9 = (f32[64,64]{0,1:T(8,128)S(1)}, f32[64,64]{0,1:T(8,128)S(1)}, u32[]{:S(2)}, u32[]{:S(2)}) collective-permute-start(f32[64,64]{0,1:T(8,128)S(1)} %add.60), channel_id=1, source_target_pairs={{0,128},{1,129},{2,130},{3,131},{4,132},{5,133},{6,134},{7,135},{8... | collective-permute-start | bytes 49160 | tf_op jit(solution)/shard_map/ppermute | solution.py:23
  118.2 7.3 %collective-permute-start.10 = (f32[64,64]{0,1:T(8,128)S(1)}, f32[64,64]{0,1:T(8,128)S(1)}, u32[]{:S(2)}, u32[]{:S(2)}) collective-permute-start(f32[64,64]{0,1:T(8,128)S(1)} %add.61), channel_id=1, source_target_pairs={{0,256},{1,257},{2,258},{3,259},{4,260},{5,261},{6,262},{7,263},{8... | collective-permute-start | bytes 49160 | tf_op jit(solution)/shard_map/ppermute | solution.py:23
where the time goes:
time: 142 us
  starting transfers between devices  42.3 us (30%)
  waiting for transfers between devices  28.5 us (20%)
  local copies, waits for them, and re-layouts  24 us (17%)
  other arithmetic  20.4 us (14%)
  blocking collectives  20.2 us (14%)
  matrix products  5.2 us (4%)
    ppermute x9, starting transfers between devices, partner_2(): return lax.ppermute(value, axis, pairs)  34.2 us
    ppermute x9, waiting for transfers between devices, partner_2(): return lax.ppermute(value, axis, pairs)  28.5 us
    all_to_all x1, blocking collectives, local(): lax.all_to_all(vorticity, 'snap', split_axis=2, concat_axis=0, tiled=True)  20.2 us
    unnamed x16, local copies, waits for them, and re-layouts  10.7 us
    another operation x3, other arithmetic, upper_factor(): return jnp.linalg.cholesky(matrix).T  6.52 us
    ppermute x1, starting transfers between devices, extended(): before = lax.ppermute(last, axis, up)  4.83 us
    another operation x2, other arithmetic, lower_solve(): return jax.scipy.linalg.solve_triangular(lower_mat, right_rows, lower=True)  4.83 us
    all_to_all x2, local copies, waits for them, and re-layouts, local(): lax.all_to_all(vorticity, 'snap', split_axis=2, concat_axis=0, tiled=True)  3.3 us
  transfers between devices with their start and end apart: 11, of which 9 were waited for; matrix products, arithmetic and copies ran while one was open for 8% of the time, Pallas kernels for 0%

commit v1 on v0

v1 whole, which is shorter than its diff:
```python
import functools

import jax
import jax.numpy as jnp
from jax import lax
from jax.experimental import pallas as pl
from jax.experimental.pallas import tpu as pltpu
from jax.sharding import PartitionSpec as P

F32 = jnp.float32
BF16 = jnp.bfloat16
VMEM = pl.BlockSpec(memory_space=pltpu.VMEM)
SMEM = pl.BlockSpec(memory_space=pltpu.SMEM)
ANY = pl.BlockSpec(memory_space=pl.ANY)
MIB = 1024 * 1024


def params(mib):
    return pltpu.CompilerParams(vmem_limit_bytes=mib * MIB)


def cost(flops, nbytes):
    return pl.CostEstimate(flops=flops, bytes_accessed=nbytes, transcendentals=0)


def edges_kernel(vel, first_ref, last_ref, head, tail, sems):
    snaps, rows = vel.shape[1], vel.shape[2]
    copies = []
    for c in range(2):
        for side, (buf, start) in enumerate(((head, 0), (tail, rows - 8))):
            src = vel.at[c, :, pl.ds(start, 8), :]
            copies.append(pltpu.make_async_copy(src, buf.at[c], sems.at[2 * c + side]))
    for copy in copies:
        copy.start()
    for c in range(2):
        for side, (buf, out) in enumerate(((head, first_ref), (tail, last_ref))):
            copies[2 * c + side].wait()
            for r in range(3):
                row = r if side == 0 else 5 + r
                for m in range(snaps):
                    out[c, r, m : m + 1, :] = buf[c, m, row : row + 1, :]


def edges(velocity):
    _, snaps, _, cols = velocity.shape
    out = jax.ShapeDtypeStruct((2, 3, snaps, cols), F32)
    return pl.pallas_call(
        edges_kernel,
        out_shape=(out, out),
        in_specs=[ANY],
        out_specs=(VMEM, VMEM),
        scratch_shapes=[
            pltpu.VMEM((2, snaps, 8, cols), F32),
            pltpu.VMEM((2, snaps, 8, cols), F32),
            pltpu.SemaphoreType.DMA((4,)),
        ],
        compiler_params=params(8),
        name="edges",
    )(velocity)


def stencil(near, middle, far):
    return 45.0 * near - 9.0 * middle + far


def vorticity_kernel(table, vel, index_ref, out_ref, edge_ref, pad, metric, sems):
    snaps, rows, cols = vel.shape[1], vel.shape[2], vel.shape[3]
    blocks = cols // 128

    def copy(c, m):
        return pltpu.make_async_copy(vel.at[c, m], pad.at[c, m, pl.ds(8, rows), :], sems.at[c, m])

    for m in range(snaps):
        for c in range(2):
            copy(c, m).start()
    zero = jnp.zeros((2, snaps, 8, cols), F32)
    pad[:, :, 0:8, :] = zero
    pad[:, :, rows + 8 : rows + 16, :] = zero
    for r in range(rows // 8):
        index = index_ref[8 * r : 8 * r + 8, :]
        bits = [(index & (1 << b)) != 0 for b in range(4)]
        for t in range(4):
            level = [table[t, k] * (1.0 / 60.0) for k in range(16)]
            for bit in bits:
                level = [
                    jnp.where(bit, level[2 * k + 1], level[2 * k]) for k in range(len(level) // 2)
                ]
            metric[t, 8 * r : 8 * r + 8, :] = level[0]
    for t, slot in ((0, 0), (2, 1)):
        edge_ref[slot, 0:8, :] = metric[t, 0:8, :]
        edge_ref[slot, 8:16, :] = metric[t, rows - 8 : rows, :]

    def snapshot(m, carry):
        for c in range(2):
            copy(c, m).wait()
        for r in range(rows // 8):
            top = 8 + 8 * r
            total = None
            for c, xi_term, eta_term, sign in ((1, 0, 1, 1.0), (0, 2, 3, -1.0)):
                span = slice(8 * r, 8 * r + 8)

                def layer(k):
                    return pad[c, m, pl.ds(top + k, 8), :]

                along = stencil(
                    layer(1) - layer(-1), layer(2) - layer(-2), layer(3) - layer(-3)
                )
                field = layer(0)

                def turned(k):
                    return pltpu.roll(field, (-k) % cols, 1)

                around = stencil(
                    turned(1) - turned(-1), turned(2) - turned(-2), turned(3) - turned(-3)
                )
                term = metric[xi_term, span, :] * along + metric[eta_term, span, :] * around
                total = term if total is None else total - term
            for p in range(blocks):
                row = pl.multiple_of(m * rows + 8 * r, 8)
                out_ref[p, pl.ds(row, 8), :] = total[:, 128 * p : 128 * p + 128]
        return carry

    lax.fori_loop(0, snaps, snapshot, 0)


def vorticity_inside(table, velocity, index):
    _, snaps, rows, cols = velocity.shape
    return pl.pallas_call(
        vorticity_kernel,
        out_shape=(
            jax.ShapeDtypeStruct((cols // 128, snaps * rows, 128), F32),
            jax.ShapeDtypeStruct((2, 16, cols), F32),
        ),
        in_specs=[SMEM, ANY, VMEM],
        out_specs=(VMEM, VMEM),
        scratch_shapes=[
            pltpu.VMEM((2, snaps, rows + 16, cols), F32),
            pltpu.VMEM((4, rows, cols), F32),
            pltpu.SemaphoreType.DMA((2, snaps)),
        ],
        compiler_params=params(24),
        cost_estimate=cost(4000000000, 4 * MIB),
        name="vorticity_inside",
    )(table, velocity, index)


def border_kernel(part_ref, before, after, edge, out_ref):
    snaps, cols = before.shape[2], before.shape[3]
    rows = part_ref.shape[1] // snaps
    weights = ((-1.0, 9.0, -45.0), (0.0, -1.0, 9.0), (0.0, 0.0, -1.0))
    out_ref[...] = part_ref[...]
    for side in range(2):
        for r in range(3):
            halo = before if side == 0 else after
            row = r if side == 0 else rows - 1 - r
            line = r if side == 0 else 15 - r
            terms = []
            for c in (1, 0):
                total = None
                for k in range(3):
                    w = weights[r][k]
                    if w != 0.0:
                        near = halo[c, k] if side == 0 else halo[c, 2 - k]
                        piece = (w if side == 0 else -w) * near
                        total = piece if total is None else total + piece
                terms.append(total)
            added = edge[0, line : line + 1, :] * terms[0] - edge[1, line : line + 1, :] * terms[1]
            for p in range(cols // 128):
                place = pl.ds(row, snaps, stride=rows)
                out_ref[p, place, :] = part_ref[p, place, :] + added[:, 128 * p : 128 * p + 128]


def with_border(part, before, after, edge):
    return pl.pallas_call(
        border_kernel,
        out_shape=jax.ShapeDtypeStruct(part.shape, F32),
        in_specs=[VMEM] * 4,
        out_specs=VMEM,
        compiler_params=params(8),
        cost_estimate=cost(1000000, MIB // 2),
        name="border",
    )(part, before, after, edge)


def split3(value):
    high = value.astype(BF16)
    rest = value - high.astype(F32)
    middle = rest.astype(BF16)
    low = (rest - middle.astype(F32)).astype(BF16)
    return high, middle, low


def gram_kernel(scale, copies, z_ref, parts_ref, gram_ref):
    snaps = parts_ref.shape[0] // 3
    rows = z_ref.shape[0] // snaps
    total = None
    for i in range(0, rows, 2):
        for k in range(2):
            for part, value in enumerate(split3(z_ref[pl.ds(i + k, snaps, stride=rows), :])):
                at = (i + k) * 128
                parts_ref[part * snaps : (part + 1) * snaps, at : at + 128] = value
        both = parts_ref[:, i * 128 : i * 128 + 256]
        dims = (((1,), (1,)), ((), ()))
        piece = lax.dot_general(both, both, dims, preferred_element_type=F32)
        total = piece if total is None else total + piece
    cut = [slice(snaps * k, snaps * (k + 1)) for k in range(3)]
    order = ((2, 2), (1, 2), (2, 1), (0, 2), (2, 0), (1, 1), (0, 1), (1, 0), (0, 0))
    gram = None
    for a, b in order:
        block = total[cut[a], cut[b]]
        gram = block if gram is None else gram + block
    gram = gram * scale
    half = snaps // 2
    packed = jnp.concatenate([gram[:half], gram[half:]], axis=1)
    for n in range(copies):
        gram_ref[n] = packed


def gram_of(z, snaps, scale, copies):
    cells = z.shape[0] // snaps * 128
    return pl.pallas_call(
        functools.partial(gram_kernel, scale, copies),
        out_shape=(
            jax.ShapeDtypeStruct((3 * snaps, cells), BF16),
            jax.ShapeDtypeStruct((copies, snaps // 2, 2 * snaps), F32),
        ),
        in_specs=[VMEM],
        out_specs=(VMEM, VMEM),
        compiler_params=params(16),
        name="gram",
    )(z)


def added(values):
    total = values[0]
    for n in range(1, values.shape[0]):
        total = total + values[n]
    return total


def sum_kernel(in_ref, out_ref):
    total = added(in_ref)
    for n in range(out_ref.shape[0]):
        out_ref[n] = total


def summed(arrived, copies):
    return pl.pallas_call(
        sum_kernel,
        out_shape=jax.ShapeDtypeStruct((copies,) + arrived.shape[1:], F32),
        in_specs=[VMEM],
        out_specs=VMEM,
        compiler_params=params(4),
        name="summed",
    )(arrived)


def eliminate(rows):
    count = len(rows)
    sub = lax.broadcasted_iota(jnp.int32, (8, 128), 0)
    for b in range(count):
        cols = {
            v: [jnp.broadcast_to(rows[v][:, 8 * b + j : 8 * b + j + 1], (8, 128)) for j in range(8)]
            for v in range(b, count)
        }
        pivots = None
        for j in range(8):
            pivot = jnp.broadcast_to(cols[b][j][j : j + 1, :], (8, 128))
            pivots = pivot if pivots is None else jnp.where(sub == j, pivot, pivots)
            inverse = 1.0 / pivot
            lead = [jnp.broadcast_to(cols[b][jj][j : j + 1, :], (8, 128)) for jj in range(8)]
            lead_row = jnp.broadcast_to(rows[b][j : j + 1, :], (8, 128))
            for v in range(b, count):
                factor = cols[v][j] * inverse
                if v == b:
                    factor = jnp.where(sub > j, factor, 0.0)
                for jj in range(j + 1, 8):
                    cols[v][jj] = cols[v][jj] - factor * lead[jj]
                rows[v] = rows[v] - factor * lead_row
        root = lax.rsqrt(pivots)
        root = root * (1.5 - 0.5 * pivots * root * root)
        rows[b] = rows[b] * root
    return rows


def modes_kernel(sum_ref, parts_ref, mode_ref, operator_ref):
    half = sum_ref.shape[1]
    snaps = 2 * half
    less = snaps - 1
    packed = added(sum_ref)
    lane = lax.broadcasted_iota(jnp.int32, (8, 128), 1)
    sub = lax.broadcasted_iota(jnp.int32, (8, 128), 0)
    rows = []
    for v in range(snaps // 8):
        if v < half // 8:
            block = packed[8 * v : 8 * v + 8]
        else:
            block = pltpu.roll(packed[8 * v - half : 8 * v - half + 8], 128 - snaps, 1)
        one = jnp.where(lane == snaps + 8 * v + sub, 1.0, 0.0)
        rows.append(jnp.where(lane < snaps, block, one))
    rows = eliminate(rows)
    couple, inverse, left = [], [], []
    for v in range(snaps // 8):
        upper = jnp.where((lane < snaps) & (lane < 8 * v + sub), 0.0, rows[v])
        turned = pltpu.roll(upper, 127, 1)
        couple.append(jnp.where(lane < less, turned, 0.0)[:, :snaps])
        turned = pltpu.roll(rows[v], 128 - snaps, 1)
        inverse.append(jnp.where(lane < less, turned, 0.0)[:, :snaps])
        turned = pltpu.roll(rows[v], 128 - snaps + 1, 1)
        left.append(jnp.where((lane > 0) & (lane < snaps), turned, 0.0)[:, :snaps])
    parts = split3(jnp.concatenate(left, axis=0))
    wide = jnp.concatenate([jnp.concatenate([part] * 3, axis=1) for part in parts], axis=0)
    for i in range(0, parts_ref.shape[1] // 128, 2):
        product = jnp.dot(wide, parts_ref[:, i * 128 : i * 128 + 256], preferred_element_type=F32)
        result = product[2 * snaps :] + product[snaps : 2 * snaps] + product[:snaps]
        for k in range(2):
            place = pl.ds(i + k, less, stride=mode_ref.shape[0] // less)
            mode_ref[place, :] = result[:less, 128 * k : 128 * k + 128]
    operator = lax.dot_general(
        jnp.concatenate(couple, axis=0),
        jnp.concatenate(inverse, axis=0),
        (((1,), (1,)), ((), ())),
        precision=lax.Precision.HIGHEST,
        preferred_element_type=F32,
    )
    operator_ref[...] = operator[:less, :less]


def modes_of(arrived, parts):
    snaps = 2 * arrived.shape[1]
    rows = parts.shape[1] // 128
    return pl.pallas_call(
        modes_kernel,
        out_shape=(
            jax.ShapeDtypeStruct(((snaps - 1) * rows, 128), F32),
            jax.ShapeDtypeStruct((snaps - 1, snaps - 1), F32),
        ),
        in_specs=[VMEM, VMEM],
        out_specs=(VMEM, VMEM),
        compiler_params=params(16),
        name="modes",
    )(arrived, parts)


def space_groups(size):
    if size <= 8:
        return [None]
    inner = 8
    near = [[a * inner + b for b in range(inner)] for a in range(size // inner)]
    far = [[a * inner + b for a in range(size // inner)] for b in range(inner)]
    return [near, far]


def local(velocity, index, table):
    size, snap_devices = lax.axis_size("space"), lax.axis_size("snap")
    _, snaps, rows, cols = velocity.shape
    first, last = edges(velocity)
    up = [(i, i + 1) for i in range(size - 1)]
    down = [(i + 1, i) for i in range(size - 1)]
    before = lax.ppermute(last, "space", up)
    after = lax.ppermute(first, "space", down)
    part, edge = vorticity_inside(table, velocity, index)
    whole = with_border(part, before, after, edge)
    owned = lax.all_to_all(whole, "snap", 0, 0)
    all_snaps = snaps * snap_devices
    z = owned.reshape(all_snaps * rows, 128)
    scale = 1.0 / (rows * size * cols)
    stages = [("snap", None, snap_devices)]
    for groups in space_groups(size):
        stages.append(("space", groups, size if groups is None else len(groups[0])))
    parts, sent = gram_of(z, all_snaps, scale, stages[0][2])
    for n, (axis, groups, _) in enumerate(stages):
        arrived = lax.all_to_all(sent, axis, 0, 0, axis_index_groups=groups)
        if n + 1 < len(stages):
            sent = summed(arrived, stages[n + 1][2])
    mode, operator = modes_of(arrived, parts)
    return mode.reshape(all_snaps - 1, rows, 128), operator


def solution(mesh):
    in_specs = (P(None, "snap", "space", None), P("space", None), P())
    out_specs = (P(None, "space", "snap"), P())
    return jax.shard_map(local, mesh=mesh, in_specs=in_specs, out_specs=out_specs, check_vma=False)
```

time: 142 us -> 87.1 us (0.61)
  the two profiles are of different devices: /device:TPU:56 before, /device:TPU:2 now
where the time goes in v1:
time: 87.1 us; the launch traced here: 86.8 us
  blocking collectives  65.2 us (75%)
  Pallas kernels  13.4 us (15%)
  starting transfers between devices  4.92 us (6%)
  local copies, waits for them, and re-layouts  2.49 us (3%)
    all_to_all x3, blocking collectives, local(): arrived = lax.all_to_all(sent, axis, 0, 0, axis_index_groups=groups)  44.4 us
    all_to_all x1, blocking collectives, local(): owned = lax.all_to_all(whole, 'snap', 0, 0)  20.8 us
    pallas_call x1, Pallas kernels, vorticity_inside(): pl.pallas_call(vorticity_kernel, out_shape=(jax.ShapeDtypeStruct((cols //...  7.74 us
    pallas_call x1, Pallas kernels, modes_of(): pl.pallas_call(modes_kernel, out_shape=(jax.ShapeDtypeStruct(((snaps - 1)...  3.72 us
    ppermute x1, starting transfers between devices, local(): before = lax.ppermute(last, 'space', up)  3.62 us
    unnamed x8, local copies, waits for them, and re-layouts  2.49 us
  transfers between devices with their start and end apart: 2, of which 0 were waited for; matrix products, arithmetic and copies ran while one was open for 0% of the time, Pallas kernels for 9%

profile of v1, /device:TPU:2, one launch (start us, length us, event | category | flops | bytes accessed | tf_op | source)
XLA Modules:
  0.0 86.8 jit_solution(7184818857945617212)
XLA Ops:
  0.6 0.0 copy-start
  0.6 1.6 %copy-done = f32[2,8,32,1024]{3,2,1,0:T(8,128)S(1)} copy-done((f32[2,8,32,1024]{3,2,1,0:T(8,128)S(1)}, f32[2,8,32,1024]{3,2,1,0:T(8,128)}, u32[]{:S(2)}) %copy-start) | copy-done | bytes 2097176
  2.2 0.0 copy-start.1
  2.2 0.0 copy-start.3
  2.2 0.2 edges.1
  2.4 3.6 %collective-permute-start = (f32[2,3,8,1024]{3,2,1,0:T(8,128)S(1)}, f32[2,3,8,1024]{3,2,1,0:T(8,128)S(1)}, u32[]{:S(2)}, u32[]{:S(2)}) collective-permute-start(f32[2,3,8,1024]{3,2,1,0:T(8,128)S(1)} %get-tuple-element.11), channel_id=1, source_target_pairs={{0,1},{1,2},{2,3},{3,4},{4,5},{5,6},{6,7},{7,8},{8,9},{9,10},{10,1... | collective-permute-start | bytes 589832 | tf_op jit(solution)/shard_map/ppermute | solution.py:360
  6.1 1.3 %collective-permute-start.1 = (f32[2,3,8,1024]{3,2,1,0:T(8,128)S(1)}, f32[2,3,8,1024]{3,2,1,0:T(8,128)S(1)}, u32[]{:S(2)}, u32[]{:S(2)}) collective-permute-start(f32[2,3,8,1024]{3,2,1,0:T(8,128)S(1)} %get-tuple-element.12), channel_id=1, source_target_pairs={{1,0},{2,1},{3,2},{4,3},{5,4},{6,5},{7,6},{8,7},{9,8},{10,9},{11,1... | collective-permute-start | bytes 589832 | tf_op jit(solution)/shard_map/ppermute | solution.py:361
  7.4 0.0 copy-done.1
  7.4 0.0 copy-done.3
  7.4 0.0 copy-start.2
  7.4 0.9 %copy-done.2 = s32[32,1024]{1,0:T(8,128)S(1)} copy-done((s32[32,1024]{1,0:T(8,128)S(1)}, s32[32,1024]{1,0:T(8,128)}, u32[]{:S(2)}) %copy-start.2) | copy-done | bytes 131096
  8.3 7.7 %vorticity_inside.1 = (f32[8,256,128]{2,1,0:T(8,128)S(1)}, f32[2,16,1024]{2,1,0:T(8,128)S(1)}) custom-call(f32[4,16]{1,0:T(4,128)S(1)} %copy-done.3, f32[2,8,32,1024]{3,2,1,0:T(8,128)S(1)} %copy-done.1, s32[32,1024]{1,0:T(8,128)S(1)} %copy-done.2), custom_call_target="tpu_custom_call" | custom-call | flops 4000000000 | bytes 4194304 | tf_op jit(solution)/shard_map/vorticity_inside/pallas_call | solution.py:128
  16.1 0.0 collective-permute-done.before
  16.1 0.0 collective-permute-done.1.after
  16.1 0.3 border.1
  16.4 20.8 %all_to_all.20 = f32[8,256,128]{2,1,0:T(8,128)S(1)} all-to-all(f32[8,256,128]{2,1,0:T(8,128)S(1)} %border.1), channel_id=1, replica_groups=mesh['snap'=8,'space'=64] {'snap'}, dimensions={0} | all-to-all | bytes 2097152 | tf_op jit(solution)/shard_map/all_to_all | solution.py:364
  37.2 1.3 %gram.1 = (bf16[192,4096]{1,0:T(8,128)(2,1)S(1)}, f32[8,32,128]{2,1,0:T(8,128)S(1)}) custom-call(f32[2048,128]{1,0:T(8,128)S(1)} %bitcast.2), custom_call_target="tpu_custom_call" | custom-call | tf_op jit(solution)/shard_map/gram/pallas_call | solution.py:221
  38.6 8.5 %all_to_all.21.in_ref = f32[8,32,128]{2,1,0:T(8,128)S(1)} all-to-all(f32[8,32,128]{2,1,0:T(8,128)S(1)} %get-tuple-element.14), channel_id=1, replica_groups=mesh['snap'=8,'space'=64] {'snap'}, dimensions={0} | all-to-all | bytes 262144 | tf_op jit(solution)/shard_map/all_to_all | solution.py:373
  47.1 16.7 %all_to_all.22.in_ref = f32[8,32,128]{2,1,0:T(8,128)S(1)} all-to-all(f32[8,32,128]{2,1,0:T(8,128)S(1)} %summed.2), channel_id=1, replica_groups={{0,1,2,3,4,5,6,7},{8,9,10,11,12,13,14,15},{16,17,18,19,20,21,22,23},{24..., dimensions={0} | all-to-all | bytes 262144 | tf_op jit(solution)/shard_map/all_to_all | solution.py:373
  63.9 19.2 %all_to_all.23.sum_ref = f32[8,32,128]{2,1,0:T(8,128)S(1)} all-to-all(f32[8,32,128]{2,1,0:T(8,128)S(1)} %summed.3), channel_id=1, replica_groups={{0,8,16,24,32,40,48,56},{1,9,17,25,33,41,49,57},{2,10,18,26,34,42,50,58..., dimensions={0} | all-to-all | bytes 262144 | tf_op jit(solution)/shard_map/all_to_all | solution.py:373
  83.0 3.7 %modes.1 = (f32[2016,128]{1,0:T(8,128)}, f32[63,63]{1,0:T(8,128)}) custom-call(f32[8,32,128]{2,1,0:T(8,128)S(1)} %all_to_all.23.sum_ref, bf16[192,4096]{1,0:T(8,128)(2,1)S(1)} %get-tuple-element.15.parts_ref), custom_call_target="tpu_custom_call" | custom-call | tf_op jit(solution)/shard_map/modes/pallas_call | solution.py:332
  (2 shorter events, 0.0 us)
Async XLA Ops:
  0.6 1.6 %copy-start = (f32[2,8,32,1024]{3,2,1,0:T(8,128)S(1)}, f32[2,8,32,1024]{3,2,1,0:T(8,128)}, u32[]{:S(2)}) copy-start(f32[2,8,32,1024]{3,2,1,0:T(8,128)} %vel.3) | copy-start | bytes 6291460
  2.2 5.2 %copy-start.1 = (f32[2,8,32,1024]{3,2,1,0:T(8,128)S(1)}, f32[2,8,32,1024]{3,2,1,0:T(8,128)}, u32[]{:S(2)}) copy-start(f32[2,8,32,1024]{3,2,1,0:T(8,128)} %vel.3) | copy-start | bytes 6291460
  2.2 5.2 %copy-start.3 = (f32[4,16]{1,0:T(4,128)S(1)}, f32[4,16]{1,0:T(4,128)}, u32[]{:S(2)}) copy-start(f32[4,16]{1,0:T(4,128)} %table.1) | copy-start | bytes 772
  2.4 13.6 %collective-permute-start = (f32[2,3,8,1024]{3,2,1,0:T(8,128)S(1)}, f32[2,3,8,1024]{3,2,1,0:T(8,128)S(1)}, u32[]{:S(2)}, u32[]{:S(2)}) collective-permute-start(f32[2,3,8,1024]{3,2,1,0:T(8,128)S(1)} %get-tuple-element.11), channel_id=1, source_target_pairs={{0,1},{1,2},{2,3},{3,4},{4,5},{5,6},{6,7},{7,8},{8,9},{9,10},{10,1... | collective-permute-start | bytes 589832 | tf_op jit(solution)/shard_map/ppermute | solution.py:360
  6.1 10.0 %collective-permute-start.1 = (f32[2,3,8,1024]{3,2,1,0:T(8,128)S(1)}, f32[2,3,8,1024]{3,2,1,0:T(8,128)S(1)}, u32[]{:S(2)}, u32[]{:S(2)}) collective-permute-start(f32[2,3,8,1024]{3,2,1,0:T(8,128)S(1)} %get-tuple-element.12), channel_id=1, source_target_pairs={{1,0},{2,1},{3,2},{4,3},{5,4},{6,5},{7,6},{8,7},{9,8},{10,9},{11,1... | collective-permute-start | bytes 589832 | tf_op jit(solution)/shard_map/ppermute | solution.py:361
  7.4 0.9 %copy-start.2 = (s32[32,1024]{1,0:T(8,128)S(1)}, s32[32,1024]{1,0:T(8,128)}, u32[]{:S(2)}) copy-start(s32[32,1024]{1,0:T(8,128)} %index_ref.1) | copy-start | bytes 393220

commit v2 on v1

--- a/solution.py
+++ b/solution.py
@@ -11,7 +11,7 @@
 BF16 = jnp.bfloat16
 VMEM = pl.BlockSpec(memory_space=pltpu.VMEM)
 SMEM = pl.BlockSpec(memory_space=pltpu.SMEM)
-ANY = pl.BlockSpec(memory_space=pl.ANY)
+HBM = pl.BlockSpec(memory_space=pltpu.HBM)
 MIB = 1024 * 1024
 
 
@@ -47,14 +47,14 @@
     return pl.pallas_call(
         edges_kernel,
         out_shape=(out, out),
-        in_specs=[ANY],
+        in_specs=[HBM],
         out_specs=(VMEM, VMEM),
         scratch_shapes=[
             pltpu.VMEM((2, snaps, 8, cols), F32),
             pltpu.VMEM((2, snaps, 8, cols), F32),
             pltpu.SemaphoreType.DMA((4,)),
         ],
-        compiler_params=params(8),
+        compiler_params=params(52),
         name="edges",
     )(velocity)
 
@@ -63,97 +63,118 @@
     return 45.0 * near - 9.0 * middle + far
 
 
-def vorticity_kernel(table, vel, index_ref, out_ref, edge_ref, pad, metric, sems):
-    snaps, rows, cols = vel.shape[1], vel.shape[2], vel.shape[3]
-    blocks = cols // 128
-
-    def copy(c, m):
-        return pltpu.make_async_copy(vel.at[c, m], pad.at[c, m, pl.ds(8, rows), :], sems.at[c, m])
-
-    for m in range(snaps):
+def metric_of(table, index):
+    bits = [(index & (1 << b)) != 0 for b in range(4)]
+    terms = []
+    for t in range(4):
+        level = [table[t, k] * (1.0 / 60.0) for k in range(16)]
+        for bit in bits:
+            level = [jnp.where(bit, level[2 * k + 1], level[2 * k]) for k in range(len(level) // 2)]
+        terms.append(level[0])
+    return terms
+
+
+def vorticity_kernel(table, vel, index_hbm, out_ref, edge_ref, raw, lines, index_ref, sems, index_sem):
+    rows, cols = index_hbm.shape
+    snaps, blocks = vel.shape[1] // rows, cols // 128
+    lane = lax.broadcasted_iota(jnp.int32, (8, 128), 1)
+    copies = {}
+    for p in range(blocks):
         for c in range(2):
-            copy(c, m).start()
-    zero = jnp.zeros((2, snaps, 8, cols), F32)
-    pad[:, :, 0:8, :] = zero
-    pad[:, :, rows + 8 : rows + 16, :] = zero
-    for r in range(rows // 8):
-        index = index_ref[8 * r : 8 * r + 8, :]
-        bits = [(index & (1 << b)) != 0 for b in range(4)]
-        for t in range(4):
-            level = [table[t, k] * (1.0 / 60.0) for k in range(16)]
-            for bit in bits:
-                level = [
-                    jnp.where(bit, level[2 * k + 1], level[2 * k]) for k in range(len(level) // 2)
-                ]
-            metric[t, 8 * r : 8 * r + 8, :] = level[0]
-    for t, slot in ((0, 0), (2, 1)):
-        edge_ref[slot, 0:8, :] = metric[t, 0:8, :]
-        edge_ref[slot, 8:16, :] = metric[t, rows - 8 : rows, :]
-
-    def snapshot(m, carry):
+            src = vel.at[c, :, pl.ds(128 * p, 128)]
+            copies[c, p] = pltpu.make_async_copy(src, raw.at[c, p], sems.at[c, p])
+            copies[c, p].start()
+    index_copy = pltpu.make_async_copy(index_hbm, index_ref, index_sem)
+    index_copy.start()
+    zero = jnp.zeros((2, 3, snaps, cols), F32)
+    lines[:, 0:3] = zero
+    lines[:, rows + 3 : rows + 6] = zero
+    for p in range(blocks):
         for c in range(2):
-            copy(c, m).wait()
-        for r in range(rows // 8):
-            top = 8 + 8 * r
-            total = None
-            for c, xi_term, eta_term, sign in ((1, 0, 1, 1.0), (0, 2, 3, -1.0)):
-                span = slice(8 * r, 8 * r + 8)
-
-                def layer(k):
-                    return pad[c, m, pl.ds(top + k, 8), :]
-
-                along = stencil(
-                    layer(1) - layer(-1), layer(2) - layer(-2), layer(3) - layer(-3)
-                )
-                field = layer(0)
-
-                def turned(k):
-                    return pltpu.roll(field, (-k) % cols, 1)
-
-                around = stencil(
-                    turned(1) - turned(-1), turned(2) - turned(-2), turned(3) - turned(-3)
-                )
-                term = metric[xi_term, span, :] * along + metric[eta_term, span, :] * around
-                total = term if total is None else total - term
+            copies[c, p].wait()
+            for i in range(rows):
+                tile = raw[c, p, pl.ds(i, snaps, stride=rows), :]
+                lines[c, i + 3, :, 128 * p : 128 * p + 128] = tile
+
+    index_copy.wait()
+
+    def band(r, carry):
+        top = pl.multiple_of(8 * r, 8)
+        metric = []
+        for p in range(blocks):
+            index = index_ref[pl.ds(top, 8), 128 * p : 128 * p + 128]
+            metric.append(metric_of(table, index))
+
+        for s in range(8):
+            i = top + s + 3
+            total = [None] * blocks
+            for c, xi_term, eta_term in ((1, 0, 1), (0, 2, 3)):
+                field = [lines[c, i, :, 128 * p : 128 * p + 128] for p in range(blocks)]
+                left = {k: [pltpu.roll(f, 128 - k, 1) for f in field] for k in (1, 2, 3)}
+                right = {k: [pltpu.roll(f, k, 1) for f in field] for k in (1, 2, 3)}
+                for p in range(blocks):
+                    span = slice(128 * p, 128 * p + 128)
+                    along = stencil(
+                        lines[c, i + 1, :, span] - lines[c, i - 1, :, span],
+                        lines[c, i + 2, :, span] - lines[c, i - 2, :, span],
+                        lines[c, i + 3, :, span] - lines[c, i - 3, :, span],
+                    )
+                    diffs = []
+                    for k in (1, 2, 3):
+                        ahead = jnp.where(
+                            lane < 128 - k, left[k][p], left[k][(p + 1) % blocks]
+                        )
+                        behind = jnp.where(lane >= k, right[k][p], right[k][(p - 1) % blocks])
+                        diffs.append(ahead - behind)
+                    around = stencil(*diffs)
+                    term = (
+                        metric[p][xi_term][s : s + 1] * along
+                        + metric[p][eta_term][s : s + 1] * around
+                    )
+                    total[p] = term if total[p] is None else total[p] - term
             for p in range(blocks):
-                row = pl.multiple_of(m * rows + 8 * r, 8)
-                out_ref[p, pl.ds(row, 8), :] = total[:, 128 * p : 128 * p + 128]
+                out_ref[p, top + s] = total[p]
+
+        for slot, t in ((0, 0), (1, 2)):
+            for p in range(blocks):
+                edge_ref[slot, pl.ds(top, 8), 128 * p : 128 * p + 128] = metric[p][t]
         return carry
 
-    lax.fori_loop(0, snaps, snapshot, 0)
+    lax.fori_loop(0, rows // 8, band, 0)
 
 
 def vorticity_inside(table, velocity, index):
     _, snaps, rows, cols = velocity.shape
+    flat = velocity.reshape(2, snaps * rows, cols)
     return pl.pallas_call(
         vorticity_kernel,
         out_shape=(
-            jax.ShapeDtypeStruct((cols // 128, snaps * rows, 128), F32),
-            jax.ShapeDtypeStruct((2, 16, cols), F32),
+            jax.ShapeDtypeStruct((cols // 128, rows, snaps, 128), F32),
+            jax.ShapeDtypeStruct((2, rows, cols), F32),
         ),
-        in_specs=[SMEM, ANY, VMEM],
+        in_specs=[SMEM, HBM, HBM],
         out_specs=(VMEM, VMEM),
         scratch_shapes=[
-            pltpu.VMEM((2, snaps, rows + 16, cols), F32),
-            pltpu.VMEM((4, rows, cols), F32),
-            pltpu.SemaphoreType.DMA((2, snaps)),
+            pltpu.VMEM((2, cols // 128, snaps * rows, 128), F32),
+            pltpu.VMEM((2, rows + 6, snaps, cols), F32),
+            pltpu.VMEM((rows, cols), jnp.int32),
+            pltpu.SemaphoreType.DMA((2, cols // 128)),
+            pltpu.SemaphoreType.DMA,
         ],
-        compiler_params=params(24),
+        compiler_params=params(52),
         cost_estimate=cost(4000000000, 4 * MIB),
         name="vorticity_inside",
-    )(table, velocity, index)
+    )(table, flat, index)
 
 
 def border_kernel(part_ref, before, after, edge, out_ref):
-    snaps, cols = before.shape[2], before.shape[3]
-    rows = part_ref.shape[1] // snaps
+    rows, cols = part_ref.shape[1], before.shape[3]
     weights = ((-1.0, 9.0, -45.0), (0.0, -1.0, 9.0), (0.0, 0.0, -1.0))
-    out_ref[...] = part_ref[...]
+    out_ref[:, 3 : rows - 3] = part_ref[:, 3 : rows - 3]
     for side in range(2):
         for r in range(3):
             halo = before if side == 0 else after
             row = r if side == 0 else rows - 1 - r
-            line = r if side == 0 else 15 - r
             terms = []
             for c in (1, 0):
                 total = None
@@ -164,10 +185,9 @@
                         piece = (w if side == 0 else -w) * near
                         total = piece if total is None else total + piece
                 terms.append(total)
-            added = edge[0, line : line + 1, :] * terms[0] - edge[1, line : line + 1, :] * terms[1]
+            more = edge[0, row : row + 1, :] * terms[0] - edge[1, row : row + 1, :] * terms[1]
             for p in range(cols // 128):
-                place = pl.ds(row, snaps, stride=rows)
-                out_ref[p, place, :] = part_ref[p, place, :] + added[:, 128 * p : 128 * p + 128]
+                out_ref[p, row] = part_ref[p, row] + more[:, 128 * p : 128 * p + 128]
 
 
 def with_border(part, before, after, edge):
@@ -191,12 +211,11 @@
 
 
 def gram_kernel(scale, copies, z_ref, parts_ref, gram_ref):
-    snaps = parts_ref.shape[0] // 3
-    rows = z_ref.shape[0] // snaps
+    snaps, rows = parts_ref.shape[0] // 3, z_ref.shape[1]
     total = None
     for i in range(0, rows, 2):
         for k in range(2):
-            for part, value in enumerate(split3(z_ref[pl.ds(i + k, snaps, stride=rows), :])):
+            for part, value in enumerate(split3(z_ref[:, i + k].reshape(snaps, 128))):
                 at = (i + k) * 128
                 parts_ref[part * snaps : (part + 1) * snaps, at : at + 128] = value
         both = parts_ref[:, i * 128 : i * 128 + 256]
@@ -216,8 +235,8 @@
         gram_ref[n] = packed
 
 
-def gram_of(z, snaps, scale, copies):
-    cells = z.shape[0] // snaps * 128
+def gram_of(z, scale, copies):
+    snaps, cells = z.shape[0] * z.shape[2], z.shape[1] * z.shape[3]
     return pl.pallas_call(
         functools.partial(gram_kernel, scale, copies),
         out_shape=(
@@ -363,12 +382,11 @@
     whole = with_border(part, before, after, edge)
     owned = lax.all_to_all(whole, "snap", 0, 0)
     all_snaps = snaps * snap_devices
-    z = owned.reshape(all_snaps * rows, 128)
     scale = 1.0 / (rows * size * cols)
     stages = [("snap", None, snap_devices)]
     for groups in space_groups(size):
         stages.append(("space", groups, size if groups is None else len(groups[0])))
-    parts, sent = gram_of(z, all_snaps, scale, stages[0][2])
+    parts, sent = gram_of(owned, scale, stages[0][2])
     for n, (axis, groups, _) in enumerate(stages):
         arrived = lax.all_to_all(sent, axis, 0, 0, axis_index_groups=groups)
         if n + 1 < len(stages):

time: 87.1 us -> 83.7 us (0.961)
  local copies, waits for them, and re-layouts: 2.49 us -> 0.01 us
    unnamed x8 -> x4, local copies, waits for them, and re-layouts: 2.49 us -> 0.01 us
    pallas_call x1, Pallas kernels: 7.74 us -> 6.67 us  [vorticity_inside(): pl.pallas_call(vorticity_kernel, out_shape=(jax.ShapeDtypeStruct((cols //...]
    pallas_call x1, Pallas kernels: 0.21 us -> 1.29 us  [edges(): pl.pallas_call(edges_kernel, out_shape=(out, out), in_specs=[HBM], out_sp...]
  transfers between devices with their start and end apart: 2 -> 2, of which waited for: 0 -> 1; matrix products, arithmetic and copies ran while one was open for 0% -> 0% of each run, Pallas kernels for 9% -> 8%
where the time goes in v2:
time: 83.7 us; the launch traced here: 83.4 us
  blocking collectives  65 us (78%)
  Pallas kernels  12.6 us (15%)
  starting transfers between devices  4.78 us (6%)
    all_to_all x3, blocking collectives, local(): arrived = lax.all_to_all(sent, axis, 0, 0, axis_index_groups=groups)  44.5 us
    all_to_all x1, blocking collectives, local(): owned = lax.all_to_all(whole, 'snap', 0, 0)  20.6 us
    pallas_call x1, Pallas kernels, vorticity_inside(): pl.pallas_call(vorticity_kernel, out_shape=(jax.ShapeDtypeStruct((cols //...  6.67 us
    pallas_call x1, Pallas kernels, modes_of(): pl.pallas_call(modes_kernel, out_shape=(jax.ShapeDtypeStruct(((snaps - 1)...  3.72 us
    ppermute x1, starting transfers between devices, local(): before = lax.ppermute(last, 'space', up)  3.49 us
  transfers between devices with their start and end apart: 2, of which 1 were waited for; matrix products, arithmetic and copies ran while one was open for 0% of the time, Pallas kernels for 8%

profile of v2, /device:TPU:2, one launch (start us, length us, event | category | flops | bytes accessed | tf_op | source)
XLA Modules:
  0.0 83.4 jit_solution(18356851013045845252)
XLA Ops:
  0.6 0.0 copy-start.1
  0.6 0.0 copy-start
  0.6 1.3 %edges.1 = (f32[2,3,8,1024]{3,2,1,0:T(8,128)S(1)}, f32[2,3,8,1024]{3,2,1,0:T(8,128)S(1)}) custom-call(f32[2,8,32,1024]{3,2,1,0:T(8,128)} %vel.1), custom_call_target="tpu_custom_call" | custom-call | tf_op jit(solution)/shard_map/edges/pallas_call | solution.py:47
  1.9 3.5 %collective-permute-start = (f32[2,3,8,1024]{3,2,1,0:T(8,128)S(1)}, f32[2,3,8,1024]{3,2,1,0:T(8,128)S(1)}, u32[]{:S(2)}, u32[]{:S(2)}) collective-permute-start(f32[2,3,8,1024]{3,2,1,0:T(8,128)S(1)} %get-tuple-element.11), channel_id=1, source_target_pairs={{0,1},{1,2},{2,3},{3,4},{4,5},{5,6},{6,7},{7,8},{8,9},{9,10},{10,1... | collective-permute-start | bytes 589832 | tf_op jit(solution)/shard_map/ppermute | solution.py:379
  5.4 1.3 %collective-permute-start.1 = (f32[2,3,8,1024]{3,2,1,0:T(8,128)S(1)}, f32[2,3,8,1024]{3,2,1,0:T(8,128)S(1)}, u32[]{:S(2)}, u32[]{:S(2)}) collective-permute-start(f32[2,3,8,1024]{3,2,1,0:T(8,128)S(1)} %get-tuple-element.12), channel_id=1, source_target_pairs={{1,0},{2,1},{3,2},{4,3},{5,4},{6,5},{7,6},{8,7},{9,8},{10,9},{11,1... | collective-permute-start | bytes 589832 | tf_op jit(solution)/shard_map/ppermute | solution.py:380
  6.7 0.0 copy-done.1
  6.8 0.0 copy-done
  6.8 6.7 %vorticity_inside.1 = (f32[8,32,8,128]{3,2,1,0:T(8,128)S(1)}, f32[2,32,1024]{2,1,0:T(8,128)S(1)}) custom-call(f32[4,16]{1,0:T(4,128)S(1)} %copy-done.1, f32[2,256,1024]{2,1,0:T(8,128)} %bitcast.2, s32[32,1024]{1,0:T(8,128)S(1)} %copy-done), custom_call_target="tpu_custom_call" | custom-call | flops 4000000000 | bytes 4194304 | tf_op jit(solution)/shard_map/vorticity_inside/pallas_call | solution.py:149
  13.4 0.0 collective-permute-done.before
  13.5 0.2 collective-permute-done.1.after
  13.7 0.1 border.1
  13.8 20.6 %all_to_all.20.z_ref = f32[8,32,8,128]{3,2,1,0:T(8,128)S(1)} all-to-all(f32[8,32,8,128]{3,2,1,0:T(8,128)S(1)} %border.1), channel_id=1, replica_groups=mesh['snap'=8,'space'=64] {'snap'}, dimensions={0} | all-to-all | bytes 2097152 | tf_op jit(solution)/shard_map/all_to_all | solution.py:383
  34.4 0.8 gram.1
  35.2 8.5 %all_to_all.21.in_ref = f32[8,32,128]{2,1,0:T(8,128)S(1)} all-to-all(f32[8,32,128]{2,1,0:T(8,128)S(1)} %get-tuple-element.14), channel_id=1, replica_groups=mesh['snap'=8,'space'=64] {'snap'}, dimensions={0} | all-to-all | bytes 262144 | tf_op jit(solution)/shard_map/all_to_all | solution.py:391
  43.7 16.7 %all_to_all.22.in_ref = f32[8,32,128]{2,1,0:T(8,128)S(1)} all-to-all(f32[8,32,128]{2,1,0:T(8,128)S(1)} %summed.2), channel_id=1, replica_groups={{0,1,2,3,4,5,6,7},{8,9,10,11,12,13,14,15},{16,17,18,19,20,21,22,23},{24..., dimensions={0} | all-to-all | bytes 262144 | tf_op jit(solution)/shard_map/all_to_all | solution.py:391
  60.5 19.2 %all_to_all.23.sum_ref = f32[8,32,128]{2,1,0:T(8,128)S(1)} all-to-all(f32[8,32,128]{2,1,0:T(8,128)S(1)} %summed.3), channel_id=1, replica_groups={{0,8,16,24,32,40,48,56},{1,9,17,25,33,41,49,57},{2,10,18,26,34,42,50,58..., dimensions={0} | all-to-all | bytes 262144 | tf_op jit(solution)/shard_map/all_to_all | solution.py:391
  79.7 3.7 %modes.1 = (f32[2016,128]{1,0:T(8,128)}, f32[63,63]{1,0:T(8,128)}) custom-call(f32[8,32,128]{2,1,0:T(8,128)S(1)} %all_to_all.23.sum_ref, bf16[192,4096]{1,0:T(8,128)(2,1)S(1)} %get-tuple-element.15.parts_ref), custom_call_target="tpu_custom_call" | custom-call | tf_op jit(solution)/shard_map/modes/pallas_call | solution.py:351
  (2 shorter events, 0.0 us)
Async XLA Ops:
  0.6 6.1 %copy-start.1 = (f32[4,16]{1,0:T(4,128)S(1)}, f32[4,16]{1,0:T(4,128)}, u32[]{:S(2)}) copy-start(f32[4,16]{1,0:T(4,128)} %table.1) | copy-start | bytes 772
  0.6 6.1 %copy-start = (s32[32,1024]{1,0:T(8,128)S(1)}, s32[32,1024]{1,0:T(8,128)}, u32[]{:S(2)}) copy-start(s32[32,1024]{1,0:T(8,128)} %index_hbm.1) | copy-start | bytes 393220
  1.9 11.5 %collective-permute-start = (f32[2,3,8,1024]{3,2,1,0:T(8,128)S(1)}, f32[2,3,8,1024]{3,2,1,0:T(8,128)S(1)}, u32[]{:S(2)}, u32[]{:S(2)}) collective-permute-start(f32[2,3,8,1024]{3,2,1,0:T(8,128)S(1)} %get-tuple-element.11), channel_id=1, source_target_pairs={{0,1},{1,2},{2,3},{3,4},{4,5},{5,6},{6,7},{7,8},{8,9},{9,10},{10,1... | collective-permute-start | bytes 589832 | tf_op jit(solution)/shard_map/ppermute | solution.py:379
  5.4 8.3 %collective-permute-start.1 = (f32[2,3,8,1024]{3,2,1,0:T(8,128)S(1)}, f32[2,3,8,1024]{3,2,1,0:T(8,128)S(1)}, u32[]{:S(2)}, u32[]{:S(2)}) collective-permute-start(f32[2,3,8,1024]{3,2,1,0:T(8,128)S(1)} %get-tuple-element.12), channel_id=1, source_target_pairs={{1,0},{2,1},{3,2},{4,3},{5,4},{6,5},{7,6},{8,7},{9,8},{10,9},{11,1... | collective-permute-start | bytes 589832 | tf_op jit(solution)/shard_map/ppermute | solution.py:380

commit v3 on v2

--- a/solution.py
+++ b/solution.py
@@ -74,94 +74,76 @@
     return terms
 
 
-def vorticity_kernel(table, vel, index_hbm, out_ref, edge_ref, raw, lines, index_ref, sems, index_sem):
-    rows, cols = index_hbm.shape
+def band_of(line, metric, out_ref, out_first, blocks):
+    lane = lax.broadcasted_iota(jnp.int32, (8, 128), 1)
+    for s in range(8):
+        total = [None] * blocks
+        for c, xi_term, eta_term in ((1, 0, 1), (0, 2, 3)):
+            field = [line(c, p, s) for p in range(blocks)]
+            for p in range(blocks):
+                span = slice(128 * p, 128 * p + 128)
+                along = stencil(
+                    line(c, p, s + 1) - line(c, p, s - 1),
+                    line(c, p, s + 2) - line(c, p, s - 2),
+                    line(c, p, s + 3) - line(c, p, s - 3),
+                )
+                after, before = field[(p + 1) % blocks], field[(p - 1) % blocks]
+                diffs = []
+                for k in (1, 2, 3):
+                    ahead = pltpu.roll(jnp.where(lane < k, after, field[p]), 128 - k, 1)
+                    behind = pltpu.roll(jnp.where(lane < 128 - k, field[p], before), k, 1)
+                    diffs.append(ahead - behind)
+                around = stencil(*diffs)
+                term = (
+                    metric[xi_term][s : s + 1, span] * along
+                    + metric[eta_term][s : s + 1, span] * around
+                )
+                total[p] = term if total[p] is None else total[p] - term
+        for p in range(blocks):
+            out_ref[p, out_first + s] = total[p]
+
+
+def vorticity_kernel(table, vel, index_ref, out_ref, edge_ref, lines):
+    rows, cols = index_ref.shape
     snaps, blocks = vel.shape[1] // rows, cols // 128
-    lane = lax.broadcasted_iota(jnp.int32, (8, 128), 1)
-    copies = {}
-    for p in range(blocks):
-        for c in range(2):
-            src = vel.at[c, :, pl.ds(128 * p, 128)]
-            copies[c, p] = pltpu.make_async_copy(src, raw.at[c, p], sems.at[c, p])
-            copies[c, p].start()
-    index_copy = pltpu.make_async_copy(index_hbm, index_ref, index_sem)
-    index_copy.start()
-    zero = jnp.zeros((2, 3, snaps, cols), F32)
-    lines[:, 0:3] = zero
-    lines[:, rows + 3 : rows + 6] = zero
-    for p in range(blocks):
-        for c in range(2):
-            copies[c, p].wait()
-            for i in range(rows):
-                tile = raw[c, p, pl.ds(i, snaps, stride=rows), :]
-                lines[c, i + 3, :, 128 * p : 128 * p + 128] = tile
-
-    index_copy.wait()
+    zero = jnp.zeros((2, blocks, 3 * snaps, 128), F32)
+    lines[:, :, : 3 * snaps] = zero
+    lines[:, :, (rows + 3) * snaps :] = zero
+    for c in range(2):
+        for m in range(snaps):
+            for r in range(0, rows, 8):
+                for p in range(blocks):
+                    tile = vel[c, m * rows + r : m * rows + r + 8, 128 * p : 128 * p + 128]
+                    lines[c, p, pl.ds((r + 3) * snaps + m, 8, stride=snaps), :] = tile
 
     def band(r, carry):
         top = pl.multiple_of(8 * r, 8)
-        metric = []
-        for p in range(blocks):
-            index = index_ref[pl.ds(top, 8), 128 * p : 128 * p + 128]
-            metric.append(metric_of(table, index))
-
-        for s in range(8):
-            i = top + s + 3
-            total = [None] * blocks
-            for c, xi_term, eta_term in ((1, 0, 1), (0, 2, 3)):
-                field = [lines[c, i, :, 128 * p : 128 * p + 128] for p in range(blocks)]
-                left = {k: [pltpu.roll(f, 128 - k, 1) for f in field] for k in (1, 2, 3)}
-                right = {k: [pltpu.roll(f, k, 1) for f in field] for k in (1, 2, 3)}
-                for p in range(blocks):
-                    span = slice(128 * p, 128 * p + 128)
-                    along = stencil(
-                        lines[c, i + 1, :, span] - lines[c, i - 1, :, span],
-                        lines[c, i + 2, :, span] - lines[c, i - 2, :, span],
-                        lines[c, i + 3, :, span] - lines[c, i - 3, :, span],
-                    )
-                    diffs = []
-                    for k in (1, 2, 3):
-                        ahead = jnp.where(
-                            lane < 128 - k, left[k][p], left[k][(p + 1) % blocks]
-                        )
-                        behind = jnp.where(lane >= k, right[k][p], right[k][(p - 1) % blocks])
-                        diffs.append(ahead - behind)
-                    around = stencil(*diffs)
-                    term = (
-                        metric[p][xi_term][s : s + 1] * along
-                        + metric[p][eta_term][s : s + 1] * around
-                    )
-                    total[p] = term if total[p] is None else total[p] - term
-            for p in range(blocks):
-                out_ref[p, top + s] = total[p]
-
-        for slot, t in ((0, 0), (1, 2)):
-            for p in range(blocks):
-                edge_ref[slot, pl.ds(top, 8), 128 * p : 128 * p + 128] = metric[p][t]
+
+        def line(c, p, s):
+            return lines[c, p, pl.ds(pl.multiple_of((top + s + 3) * snaps, 8), snaps), :]
+
+        metric = metric_of(table, index_ref[pl.ds(top, 8), :])
+        edge_ref[0, pl.ds(top, 8), :] = metric[0]
+        edge_ref[1, pl.ds(top, 8), :] = metric[2]
+        band_of(line, metric, out_ref, top, blocks)
         return carry
 
     lax.fori_loop(0, rows // 8, band, 0)
 
 
-def vorticity_inside(table, velocity, index):
-    _, snaps, rows, cols = velocity.shape
-    flat = velocity.reshape(2, snaps * rows, cols)
+def vorticity_inside(table, flat, index):
+    rows, cols = index.shape
+    snaps, blocks = flat.shape[1] // rows, cols // 128
     return pl.pallas_call(
         vorticity_kernel,
         out_shape=(
-            jax.ShapeDtypeStruct((cols // 128, rows, snaps, 128), F32),
+            jax.ShapeDtypeStruct((blocks, rows, snaps, 128), F32),
             jax.ShapeDtypeStruct((2, rows, cols), F32),
         ),
-        in_specs=[SMEM, HBM, HBM],
+        in_specs=[SMEM, VMEM, VMEM],
         out_specs=(VMEM, VMEM),
-        scratch_shapes=[
-            pltpu.VMEM((2, cols // 128, snaps * rows, 128), F32),
-            pltpu.VMEM((2, rows + 6, snaps, cols), F32),
-            pltpu.VMEM((rows, cols), jnp.int32),
-            pltpu.SemaphoreType.DMA((2, cols // 128)),
-            pltpu.SemaphoreType.DMA,
-        ],
-        compiler_params=params(52),
+        scratch_shapes=[pltpu.VMEM((2, blocks, (rows + 6) * snaps, 128), F32)],
+        compiler_params=params(16),
         cost_estimate=cost(4000000000, 4 * MIB),
         name="vorticity_inside",
     )(table, flat, index)
@@ -378,7 +360,8 @@
     down = [(i + 1, i) for i in range(size - 1)]
     before = lax.ppermute(last, "space", up)
     after = lax.ppermute(first, "space", down)
-    part, edge = vorticity_inside(table, velocity, index)
+    flat = velocity.reshape(2, snaps * rows, cols)
+    part, edge = vorticity_inside(table, flat, index)
     whole = with_border(part, before, after, edge)
     owned = lax.all_to_all(whole, "snap", 0, 0)
     all_snaps = snaps * snap_devices

time: 83.7 us -> 82.9 us (level)
  Pallas kernels: 12.6 us -> 10.9 us
  waiting for transfers between devices: 0.25 us -> 1.17 us
  blocking collectives: 65 us -> 64.1 us
  local copies, waits for them, and re-layouts: 0.01 us -> 0.91 us
    pallas_call x1, Pallas kernels: 6.67 us -> 4.84 us  [vorticity_inside(): pl.pallas_call(vorticity_kernel, out_shape=(jax.ShapeDtypeStruct((blocks,...]
    ppermute x1, waiting for transfers between devices: 0.25 us -> 1.17 us  [local(): after = lax.ppermute(first, 'space', down)]
    unnamed x4 -> x6, local copies, waits for them, and re-layouts: 0.01 us -> 0.91 us
  transfers between devices with their start and end apart: 2 -> 2, of which waited for: 1 -> 1; matrix products, arithmetic and copies ran while one was open for 0% -> 0% of each run, Pallas kernels for 8% -> 6%
where the time goes in v3:
time: 82.9 us; the launch traced here: 82.6 us
  blocking collectives  64.1 us (77%)
  Pallas kernels  10.9 us (13%)
  starting transfers between devices  4.78 us (6%)
  waiting for transfers between devices  1.17 us (1%)
  local copies, waits for them, and re-layouts  0.91 us (1%)
    all_to_all x3, blocking collectives, local(): arrived = lax.all_to_all(sent, axis, 0, 0, axis_index_groups=groups)  44 us
    all_to_all x1, blocking collectives, local(): owned = lax.all_to_all(whole, 'snap', 0, 0)  20.1 us
    pallas_call x1, Pallas kernels, vorticity_inside(): pl.pallas_call(vorticity_kernel, out_shape=(jax.ShapeDtypeStruct((blocks,...  4.84 us
    pallas_call x1, Pallas kernels, modes_of(): pl.pallas_call(modes_kernel, out_shape=(jax.ShapeDtypeStruct(((snaps - 1)...  3.72 us
    ppermute x1, starting transfers between devices, local(): before = lax.ppermute(last, 'space', up)  3.49 us
  transfers between devices with their start and end apart: 2, of which 1 were waited for; matrix products, arithmetic and copies ran while one was open for 0% of the time, Pallas kernels for 6%

profile of v3, /device:TPU:2, one launch (start us, length us, event | category | flops | bytes accessed | tf_op | source)
XLA Modules:
  0.0 82.6 jit_solution(2836773465437894783)
XLA Ops:
  0.6 0.0 copy-start
  0.6 0.0 copy-start.2
  0.6 1.4 %edges.1 = (f32[2,3,8,1024]{3,2,1,0:T(8,128)S(1)}, f32[2,3,8,1024]{3,2,1,0:T(8,128)S(1)}) custom-call(f32[2,8,32,1024]{3,2,1,0:T(8,128)} %vel.1), custom_call_target="tpu_custom_call" | custom-call | tf_op jit(solution)/shard_map/edges/pallas_call | solution.py:47
  2.1 3.5 %collective-permute-start = (f32[2,3,8,1024]{3,2,1,0:T(8,128)S(1)}, f32[2,3,8,1024]{3,2,1,0:T(8,128)S(1)}, u32[]{:S(2)}, u32[]{:S(2)}) collective-permute-start(f32[2,3,8,1024]{3,2,1,0:T(8,128)S(1)} %get-tuple-element.11), channel_id=1, source_target_pairs={{0,1},{1,2},{2,3},{3,4},{4,5},{5,6},{6,7},{7,8},{8,9},{9,10},{10,1... | collective-permute-start | bytes 589832 | tf_op jit(solution)/shard_map/ppermute | solution.py:361
  5.6 1.3 %collective-permute-start.1 = (f32[2,3,8,1024]{3,2,1,0:T(8,128)S(1)}, f32[2,3,8,1024]{3,2,1,0:T(8,128)S(1)}, u32[]{:S(2)}, u32[]{:S(2)}) collective-permute-start(f32[2,3,8,1024]{3,2,1,0:T(8,128)S(1)} %get-tuple-element.12), channel_id=1, source_target_pairs={{1,0},{2,1},{3,2},{4,3},{5,4},{6,5},{7,6},{8,7},{9,8},{10,9},{11,1... | collective-permute-start | bytes 589832 | tf_op jit(solution)/shard_map/ppermute | solution.py:362
  6.9 0.0 copy-done
  6.9 0.0 copy-done.2
  6.9 0.0 copy-start.1
  6.9 0.9 %copy-done.1 = s32[32,1024]{1,0:T(8,128)S(1)} copy-done((s32[32,1024]{1,0:T(8,128)S(1)}, s32[32,1024]{1,0:T(8,128)}, u32[]{:S(2)}) %copy-start.1) | copy-done | bytes 131096
  7.8 4.8 %vorticity_inside.1 = (f32[8,32,8,128]{3,2,1,0:T(8,128)S(1)}, f32[2,32,1024]{2,1,0:T(8,128)S(1)}) custom-call(f32[4,16]{1,0:T(4,128)S(1)} %copy-done.2, f32[2,256,1024]{2,1,0:T(8,128)S(1)} %bitcast.2, s32[32,1024]{1,0:T(8,128)S(1)} %copy-done.1), custom_call_target="tpu_custom_call" | custom-call | flops 4000000000 | bytes 4194304 | tf_op jit(solution)/shard_map/vorticity_inside/pallas_call | solution.py:137
  12.6 0.0 collective-permute-done.before
  12.6 1.2 %collective-permute-done.1.after = f32[2,3,8,1024]{3,2,1,0:T(8,128)S(1)} collective-permute-done((f32[2,3,8,1024]{3,2,1,0:T(8,128)S(1)}, f32[2,3,8,1024]{3,2,1,0:T(8,128)S(1)}, u32[]{:S(2)}, u32[]{:S(2)}) %collective-permute-start.1) | collective-permute-done | bytes 196640 | tf_op jit(solution)/shard_map/ppermute | solution.py:362
  13.8 0.1 border.1
  13.9 20.1 %all_to_all.20.z_ref = f32[8,32,8,128]{3,2,1,0:T(8,128)S(1)} all-to-all(f32[8,32,8,128]{3,2,1,0:T(8,128)S(1)} %border.1), channel_id=1, replica_groups=mesh['snap'=8,'space'=64] {'snap'}, dimensions={0} | all-to-all | bytes 2097152 | tf_op jit(solution)/shard_map/all_to_all | solution.py:366
  34.0 0.8 gram.1
  34.8 8.5 %all_to_all.21.in_ref = f32[8,32,128]{2,1,0:T(8,128)S(1)} all-to-all(f32[8,32,128]{2,1,0:T(8,128)S(1)} %get-tuple-element.14), channel_id=1, replica_groups=mesh['snap'=8,'space'=64] {'snap'}, dimensions={0} | all-to-all | bytes 262144 | tf_op jit(solution)/shard_map/all_to_all | solution.py:374
  43.4 16.3 %all_to_all.22.in_ref = f32[8,32,128]{2,1,0:T(8,128)S(1)} all-to-all(f32[8,32,128]{2,1,0:T(8,128)S(1)} %summed.2), channel_id=1, replica_groups={{0,1,2,3,4,5,6,7},{8,9,10,11,12,13,14,15},{16,17,18,19,20,21,22,23},{24..., dimensions={0} | all-to-all | bytes 262144 | tf_op jit(solution)/shard_map/all_to_all | solution.py:374
  59.7 19.2 %all_to_all.23.sum_ref = f32[8,32,128]{2,1,0:T(8,128)S(1)} all-to-all(f32[8,32,128]{2,1,0:T(8,128)S(1)} %summed.3), channel_id=1, replica_groups={{0,8,16,24,32,40,48,56},{1,9,17,25,33,41,49,57},{2,10,18,26,34,42,50,58..., dimensions={0} | all-to-all | bytes 262144 | tf_op jit(solution)/shard_map/all_to_all | solution.py:374
  78.9 3.7 %modes.1 = (f32[2016,128]{1,0:T(8,128)}, f32[63,63]{1,0:T(8,128)}) custom-call(f32[8,32,128]{2,1,0:T(8,128)S(1)} %all_to_all.23.sum_ref, bf16[192,4096]{1,0:T(8,128)(2,1)S(1)} %get-tuple-element.15.parts_ref), custom_call_target="tpu_custom_call" | custom-call | tf_op jit(solution)/shard_map/modes/pallas_call | solution.py:333
  (2 shorter events, 0.0 us)
Async XLA Ops:
  0.6 6.2 %copy-start = (f32[2,8,32,1024]{3,2,1,0:T(8,128)S(1)}, f32[2,8,32,1024]{3,2,1,0:T(8,128)}, u32[]{:S(2)}) copy-start(f32[2,8,32,1024]{3,2,1,0:T(8,128)} %vel.1) | copy-start | bytes 6291460
  0.6 6.2 %copy-start.2 = (f32[4,16]{1,0:T(4,128)S(1)}, f32[4,16]{1,0:T(4,128)}, u32[]{:S(2)}) copy-start(f32[4,16]{1,0:T(4,128)} %table.1) | copy-start | bytes 772
  2.1 10.6 %collective-permute-start = (f32[2,3,8,1024]{3,2,1,0:T(8,128)S(1)}, f32[2,3,8,1024]{3,2,1,0:T(8,128)S(1)}, u32[]{:S(2)}, u32[]{:S(2)}) collective-permute-start(f32[2,3,8,1024]{3,2,1,0:T(8,128)S(1)} %get-tuple-element.11), channel_id=1, source_target_pairs={{0,1},{1,2},{2,3},{3,4},{4,5},{5,6},{6,7},{7,8},{8,9},{9,10},{10,1... | collective-permute-start | bytes 589832 | tf_op jit(solution)/shard_map/ppermute | solution.py:361
  5.6 8.3 %collective-permute-start.1 = (f32[2,3,8,1024]{3,2,1,0:T(8,128)S(1)}, f32[2,3,8,1024]{3,2,1,0:T(8,128)S(1)}, u32[]{:S(2)}, u32[]{:S(2)}) collective-permute-start(f32[2,3,8,1024]{3,2,1,0:T(8,128)S(1)} %get-tuple-element.12), channel_id=1, source_target_pairs={{1,0},{2,1},{3,2},{4,3},{5,4},{6,5},{7,6},{8,7},{9,8},{10,9},{11,1... | collective-permute-start | bytes 589832 | tf_op jit(solution)/shard_map/ppermute | solution.py:362
  6.9 0.9 %copy-start.1 = (s32[32,1024]{1,0:T(8,128)S(1)}, s32[32,1024]{1,0:T(8,128)}, u32[]{:S(2)}) copy-start(s32[32,1024]{1,0:T(8,128)} %index_ref.1) | copy-start | bytes 393220

commit v4 on v3

--- a/solution.py
+++ b/solution.py
@@ -212,7 +212,11 @@
         gram = block if gram is None else gram + block
     gram = gram * scale
     half = snaps // 2
-    packed = jnp.concatenate([gram[:half], gram[half:]], axis=1)
+    tiles = []
+    for block in (gram[:half, :half], gram[:half, half:], gram[half:, half:]):
+        pieces = [block[8 * k : 8 * k + 8] for k in range(half // 8)]
+        tiles.append(jnp.concatenate(pieces, axis=1))
+    packed = jnp.concatenate(tiles, axis=0)
     for n in range(copies):
         gram_ref[n] = packed
 
@@ -223,7 +227,7 @@
         functools.partial(gram_kernel, scale, copies),
         out_shape=(
             jax.ShapeDtypeStruct((3 * snaps, cells), BF16),
-            jax.ShapeDtypeStruct((copies, snaps // 2, 2 * snaps), F32),
+            jax.ShapeDtypeStruct((copies, 24, 128), F32),
         ),
         in_specs=[VMEM],
         out_specs=(VMEM, VMEM),
@@ -285,18 +289,27 @@
 
 
 def modes_kernel(sum_ref, parts_ref, mode_ref, operator_ref):
-    half = sum_ref.shape[1]
-    snaps = 2 * half
-    less = snaps - 1
+    snaps = parts_ref.shape[0] // 3
+    half, less = snaps // 2, snaps - 1
     packed = added(sum_ref)
     lane = lax.broadcasted_iota(jnp.int32, (8, 128), 1)
     sub = lax.broadcasted_iota(jnp.int32, (8, 128), 0)
+    first, cross, last = packed[:8], packed[8:16], packed[16:]
+
+    def piece(tile, k, at):
+        turn = (at - half * k) % 128
+        return pltpu.roll(tile, turn, 1) if turn else tile
+
+    fill = jnp.zeros((128 - half, 128), F32)
+    cross_rows = [piece(cross, k, 0) for k in range(half // 8)]
+    crossed = jnp.concatenate(cross_rows + [fill], axis=0).T
     rows = []
     for v in range(snaps // 8):
         if v < half // 8:
-            block = packed[8 * v : 8 * v + 8]
+            block = jnp.where(lane < half, piece(first, v, 0), piece(cross, v, half))
         else:
-            block = pltpu.roll(packed[8 * v - half : 8 * v - half + 8], 128 - snaps, 1)
+            k = v - half // 8
+            block = jnp.where(lane < half, crossed[8 * k : 8 * k + 8], piece(last, k, half))
         one = jnp.where(lane == snaps + 8 * v + sub, 1.0, 0.0)
         rows.append(jnp.where(lane < snaps, block, one))
     rows = eliminate(rows)
@@ -328,8 +341,7 @@
 
 
 def modes_of(arrived, parts):
-    snaps = 2 * arrived.shape[1]
-    rows = parts.shape[1] // 128
+    snaps, rows = parts.shape[0] // 3, parts.shape[1] // 128
     return pl.pallas_call(
         modes_kernel,
         out_shape=(

time: 82.9 us -> 82 us (0.989)
  blocking collectives: 64.1 us -> 63 us
    all_to_all x3, blocking collectives: 44 us -> 43 us  [local(): arrived = lax.all_to_all(sent, axis, 0, 0, axis_index_groups=groups)]
where the time goes in v4:
time: 82 us; the launch traced here: 81.7 us
  blocking collectives  63 us (77%)
  Pallas kernels  11 us (13%)
  starting transfers between devices  4.78 us (6%)
  waiting for transfers between devices  1.17 us (1%)
  local copies, waits for them, and re-layouts  0.91 us (1%)
    all_to_all x3, blocking collectives, local(): arrived = lax.all_to_all(sent, axis, 0, 0, axis_index_groups=groups)  43 us
    all_to_all x1, blocking collectives, local(): owned = lax.all_to_all(whole, 'snap', 0, 0)  20.1 us
    pallas_call x1, Pallas kernels, vorticity_inside(): pl.pallas_call(vorticity_kernel, out_shape=(jax.ShapeDtypeStruct((blocks,...  4.84 us
    pallas_call x1, Pallas kernels, modes_of(): pl.pallas_call(modes_kernel, out_shape=(jax.ShapeDtypeStruct(((snaps - 1)...  3.84 us
    ppermute x1, starting transfers between devices, local(): before = lax.ppermute(last, 'space', up)  3.49 us
  transfers between devices with their start and end apart: 2, of which 1 were waited for; matrix products, arithmetic and copies ran while one was open for 0% of the time, Pallas kernels for 6%

profile of v4, /device:TPU:2, one launch (start us, length us, event | category | flops | bytes accessed | tf_op | source)
XLA Modules:
  0.0 81.7 jit_solution(8492061800163395058)
XLA Ops:
  0.6 0.0 copy-start
  0.6 0.0 copy-start.2
  0.6 1.4 %edges.1 = (f32[2,3,8,1024]{3,2,1,0:T(8,128)S(1)}, f32[2,3,8,1024]{3,2,1,0:T(8,128)S(1)}) custom-call(f32[2,8,32,1024]{3,2,1,0:T(8,128)} %vel.1), custom_call_target="tpu_custom_call" | custom-call | tf_op jit(solution)/shard_map/edges/pallas_call | solution.py:47
  2.1 3.5 %collective-permute-start = (f32[2,3,8,1024]{3,2,1,0:T(8,128)S(1)}, f32[2,3,8,1024]{3,2,1,0:T(8,128)S(1)}, u32[]{:S(2)}, u32[]{:S(2)}) collective-permute-start(f32[2,3,8,1024]{3,2,1,0:T(8,128)S(1)} %get-tuple-element.11), channel_id=1, source_target_pairs={{0,1},{1,2},{2,3},{3,4},{4,5},{5,6},{6,7},{7,8},{8,9},{9,10},{10,1... | collective-permute-start | bytes 589832 | tf_op jit(solution)/shard_map/ppermute | solution.py:373
  5.6 1.3 %collective-permute-start.1 = (f32[2,3,8,1024]{3,2,1,0:T(8,128)S(1)}, f32[2,3,8,1024]{3,2,1,0:T(8,128)S(1)}, u32[]{:S(2)}, u32[]{:S(2)}) collective-permute-start(f32[2,3,8,1024]{3,2,1,0:T(8,128)S(1)} %get-tuple-element.12), channel_id=1, source_target_pairs={{1,0},{2,1},{3,2},{4,3},{5,4},{6,5},{7,6},{8,7},{9,8},{10,9},{11,1... | collective-permute-start | bytes 589832 | tf_op jit(solution)/shard_map/ppermute | solution.py:374
  6.9 0.0 copy-done
  6.9 0.0 copy-done.2
  6.9 0.0 copy-start.1
  6.9 0.9 %copy-done.1 = s32[32,1024]{1,0:T(8,128)S(1)} copy-done((s32[32,1024]{1,0:T(8,128)S(1)}, s32[32,1024]{1,0:T(8,128)}, u32[]{:S(2)}) %copy-start.1) | copy-done | bytes 131096
  7.8 4.8 %vorticity_inside.1 = (f32[8,32,8,128]{3,2,1,0:T(8,128)S(1)}, f32[2,32,1024]{2,1,0:T(8,128)S(1)}) custom-call(f32[4,16]{1,0:T(4,128)S(1)} %copy-done.2, f32[2,256,1024]{2,1,0:T(8,128)S(1)} %bitcast.2, s32[32,1024]{1,0:T(8,128)S(1)} %copy-done.1), custom_call_target="tpu_custom_call" | custom-call | flops 4000000000 | bytes 4194304 | tf_op jit(solution)/shard_map/vorticity_inside/pallas_call | solution.py:137
  12.6 0.0 collective-permute-done.before
  12.6 1.2 %collective-permute-done.1.after = f32[2,3,8,1024]{3,2,1,0:T(8,128)S(1)} collective-permute-done((f32[2,3,8,1024]{3,2,1,0:T(8,128)S(1)}, f32[2,3,8,1024]{3,2,1,0:T(8,128)S(1)}, u32[]{:S(2)}, u32[]{:S(2)}) %collective-permute-start.1) | collective-permute-done | bytes 196640 | tf_op jit(solution)/shard_map/ppermute | solution.py:374
  13.8 0.1 border.1
  13.9 20.1 %all_to_all.20.z_ref = f32[8,32,8,128]{3,2,1,0:T(8,128)S(1)} all-to-all(f32[8,32,8,128]{3,2,1,0:T(8,128)S(1)} %border.1), channel_id=1, replica_groups=mesh['snap'=8,'space'=64] {'snap'}, dimensions={0} | all-to-all | bytes 2097152 | tf_op jit(solution)/shard_map/all_to_all | solution.py:378
  34.0 0.8 gram.1
  34.8 8.2 %all_to_all.21.in_ref = f32[8,24,128]{2,1,0:T(8,128)S(1)} all-to-all(f32[8,24,128]{2,1,0:T(8,128)S(1)} %get-tuple-element.14), channel_id=1, replica_groups=mesh['snap'=8,'space'=64] {'snap'}, dimensions={0} | all-to-all | bytes 196608 | tf_op jit(solution)/shard_map/all_to_all | solution.py:386
  43.0 15.9 %all_to_all.22.in_ref = f32[8,24,128]{2,1,0:T(8,128)S(1)} all-to-all(f32[8,24,128]{2,1,0:T(8,128)S(1)} %summed.2), channel_id=1, replica_groups={{0,1,2,3,4,5,6,7},{8,9,10,11,12,13,14,15},{16,17,18,19,20,21,22,23},{24..., dimensions={0} | all-to-all | bytes 196608 | tf_op jit(solution)/shard_map/all_to_all | solution.py:386
  59.0 18.8 %all_to_all.23.sum_ref = f32[8,24,128]{2,1,0:T(8,128)S(1)} all-to-all(f32[8,24,128]{2,1,0:T(8,128)S(1)} %summed.3), channel_id=1, replica_groups={{0,8,16,24,32,40,48,56},{1,9,17,25,33,41,49,57},{2,10,18,26,34,42,50,58..., dimensions={0} | all-to-all | bytes 196608 | tf_op jit(solution)/shard_map/all_to_all | solution.py:386
  77.8 3.8 %modes.1 = (f32[2016,128]{1,0:T(8,128)}, f32[63,63]{1,0:T(8,128)}) custom-call(f32[8,24,128]{2,1,0:T(8,128)S(1)} %all_to_all.23.sum_ref, bf16[192,4096]{1,0:T(8,128)(2,1)S(1)} %get-tuple-element.15.parts_ref), custom_call_target="tpu_custom_call" | custom-call | tf_op jit(solution)/shard_map/modes/pallas_call | solution.py:345
  (2 shorter events, 0.0 us)
Async XLA Ops:
  0.6 6.2 %copy-start = (f32[2,8,32,1024]{3,2,1,0:T(8,128)S(1)}, f32[2,8,32,1024]{3,2,1,0:T(8,128)}, u32[]{:S(2)}) copy-start(f32[2,8,32,1024]{3,2,1,0:T(8,128)} %vel.1) | copy-start | bytes 6291460
  0.6 6.2 %copy-start.2 = (f32[4,16]{1,0:T(4,128)S(1)}, f32[4,16]{1,0:T(4,128)}, u32[]{:S(2)}) copy-start(f32[4,16]{1,0:T(4,128)} %table.1) | copy-start | bytes 772
  2.1 10.6 %collective-permute-start = (f32[2,3,8,1024]{3,2,1,0:T(8,128)S(1)}, f32[2,3,8,1024]{3,2,1,0:T(8,128)S(1)}, u32[]{:S(2)}, u32[]{:S(2)}) collective-permute-start(f32[2,3,8,1024]{3,2,1,0:T(8,128)S(1)} %get-tuple-element.11), channel_id=1, source_target_pairs={{0,1},{1,2},{2,3},{3,4},{4,5},{5,6},{6,7},{7,8},{8,9},{9,10},{10,1... | collective-permute-start | bytes 589832 | tf_op jit(solution)/shard_map/ppermute | solution.py:373
  5.6 8.3 %collective-permute-start.1 = (f32[2,3,8,1024]{3,2,1,0:T(8,128)S(1)}, f32[2,3,8,1024]{3,2,1,0:T(8,128)S(1)}, u32[]{:S(2)}, u32[]{:S(2)}) collective-permute-start(f32[2,3,8,1024]{3,2,1,0:T(8,128)S(1)} %get-tuple-element.12), channel_id=1, source_target_pairs={{1,0},{2,1},{3,2},{4,3},{5,4},{6,5},{7,6},{8,7},{9,8},{10,9},{11,1... | collective-permute-start | bytes 589832 | tf_op jit(solution)/shard_map/ppermute | solution.py:374
  6.9 0.9 %copy-start.1 = (s32[32,1024]{1,0:T(8,128)S(1)}, s32[32,1024]{1,0:T(8,128)}, u32[]{:S(2)}) copy-start(s32[32,1024]{1,0:T(8,128)} %index_ref.1) | copy-start | bytes 393220

commit v5 on v4

--- a/solution.py
+++ b/solution.py
@@ -76,31 +76,28 @@
 
 def band_of(line, metric, out_ref, out_first, blocks):
     lane = lax.broadcasted_iota(jnp.int32, (8, 128), 1)
-    for s in range(8):
-        total = [None] * blocks
-        for c, xi_term, eta_term in ((1, 0, 1), (0, 2, 3)):
-            field = [line(c, p, s) for p in range(blocks)]
-            for p in range(blocks):
-                span = slice(128 * p, 128 * p + 128)
-                along = stencil(
-                    line(c, p, s + 1) - line(c, p, s - 1),
-                    line(c, p, s + 2) - line(c, p, s - 2),
-                    line(c, p, s + 3) - line(c, p, s - 3),
-                )
-                after, before = field[(p + 1) % blocks], field[(p - 1) % blocks]
+    for p in range(blocks):
+        span = slice(128 * p, 128 * p + 128)
+        window = [[line(c, p, s) for s in range(-3, 11)] for c in range(2)]
+        for s in range(8):
+            total = None
+            for c, xi_term, eta_term in ((1, 0, 1), (0, 2, 3)):
+                near = window[c][s : s + 7]
+                along = stencil(near[4] - near[2], near[5] - near[1], near[6] - near[0])
+                here = near[3]
+                after, before = line(c, (p + 1) % blocks, s), line(c, (p - 1) % blocks, s)
                 diffs = []
                 for k in (1, 2, 3):
-                    ahead = pltpu.roll(jnp.where(lane < k, after, field[p]), 128 - k, 1)
-                    behind = pltpu.roll(jnp.where(lane < 128 - k, field[p], before), k, 1)
+                    ahead = pltpu.roll(jnp.where(lane < k, after, here), 128 - k, 1)
+                    behind = pltpu.roll(jnp.where(lane < 128 - k, here, before), k, 1)
                     diffs.append(ahead - behind)
                 around = stencil(*diffs)
                 term = (
                     metric[xi_term][s : s + 1, span] * along
                     + metric[eta_term][s : s + 1, span] * around
                 )
-                total[p] = term if total[p] is None else total[p] - term
-        for p in range(blocks):
-            out_ref[p, out_first + s] = total[p]
+                total = term if total is None else total - term
+            out_ref[p, out_first + s] = total
 
 
 def vorticity_kernel(table, vel, index_ref, out_ref, edge_ref, lines):
@@ -117,10 +114,10 @@
                     lines[c, p, pl.ds((r + 3) * snaps + m, 8, stride=snaps), :] = tile
 
     def band(r, carry):
-        top = pl.multiple_of(8 * r, 8)
+        top = 8 * r
 
         def line(c, p, s):
-            return lines[c, p, pl.ds(pl.multiple_of((top + s + 3) * snaps, 8), snaps), :]
+            return lines[c, p, pl.ds((top + s + 3) * snaps, snaps), :]
 
         metric = metric_of(table, index_ref[pl.ds(top, 8), :])
         edge_ref[0, pl.ds(top, 8), :] = metric[0]
@@ -128,7 +125,8 @@
         band_of(line, metric, out_ref, top, blocks)
         return carry
 
-    lax.fori_loop(0, rows // 8, band, 0)
+    for r in range(rows // 8):
+        band(r, 0)
 
 
 def vorticity_inside(table, flat, index):

time: 82 us -> 81 us (0.988)
  waiting for transfers between devices: 1.17 us -> 2.1 us
  Pallas kernels: 11 us -> 10.1 us
  blocking collectives: 63 us -> 62.1 us
    ppermute x1, waiting for transfers between devices: 1.17 us -> 2.1 us  [local(): after = lax.ppermute(first, 'space', down)]
    all_to_all x3, blocking collectives: 43 us -> 42 us  [local(): arrived = lax.all_to_all(sent, axis, 0, 0, axis_index_groups=groups)]
    pallas_call x1, Pallas kernels: 4.84 us -> 3.92 us  [vorticity_inside(): pl.pallas_call(vorticity_kernel, out_shape=(jax.ShapeDtypeStruct((blocks,...]
  transfers between devices with their start and end apart: 2 -> 2, of which waited for: 1 -> 1; matrix products, arithmetic and copies ran while one was open for 0% -> 0% of each run, Pallas kernels for 6% -> 5%
where the time goes in v5:
time: 81 us; the launch traced here: 80.7 us
  blocking collectives  62.1 us (77%)
  Pallas kernels  10.1 us (12%)
  starting transfers between devices  4.78 us (6%)
  waiting for transfers between devices  2.1 us (3%)
  local copies, waits for them, and re-layouts  0.91 us (1%)
    all_to_all x3, blocking collectives, local(): arrived = lax.all_to_all(sent, axis, 0, 0, axis_index_groups=groups)  42 us
    all_to_all x1, blocking collectives, local(): owned = lax.all_to_all(whole, 'snap', 0, 0)  20.1 us
    pallas_call x1, Pallas kernels, vorticity_inside(): pl.pallas_call(vorticity_kernel, out_shape=(jax.ShapeDtypeStruct((blocks,...  3.92 us
    pallas_call x1, Pallas kernels, modes_of(): pl.pallas_call(modes_kernel, out_shape=(jax.ShapeDtypeStruct(((snaps - 1)...  3.84 us
    ppermute x1, starting transfers between devices, local(): before = lax.ppermute(last, 'space', up)  3.49 us
    ppermute x1, waiting for transfers between devices, local(): after = lax.ppermute(first, 'space', down)  2.1 us
  transfers between devices with their start and end apart: 2, of which 1 were waited for; matrix products, arithmetic and copies ran while one was open for 0% of the time, Pallas kernels for 5%

profile of v5, /device:TPU:2, one launch (start us, length us, event | category | flops | bytes accessed | tf_op | source)
XLA Modules:
  0.0 80.7 jit_solution(16807441802119586540)
XLA Ops:
  0.6 0.0 copy-start
  0.6 0.0 copy-start.2
  0.6 1.4 %edges.1 = (f32[2,3,8,1024]{3,2,1,0:T(8,128)S(1)}, f32[2,3,8,1024]{3,2,1,0:T(8,128)S(1)}) custom-call(f32[2,8,32,1024]{3,2,1,0:T(8,128)} %vel.1), custom_call_target="tpu_custom_call" | custom-call | tf_op jit(solution)/shard_map/edges/pallas_call | solution.py:47
  2.1 3.5 %collective-permute-start = (f32[2,3,8,1024]{3,2,1,0:T(8,128)S(1)}, f32[2,3,8,1024]{3,2,1,0:T(8,128)S(1)}, u32[]{:S(2)}, u32[]{:S(2)}) collective-permute-start(f32[2,3,8,1024]{3,2,1,0:T(8,128)S(1)} %get-tuple-element.11), channel_id=1, source_target_pairs={{0,1},{1,2},{2,3},{3,4},{4,5},{5,6},{6,7},{7,8},{8,9},{9,10},{10,1... | collective-permute-start | bytes 589832 | tf_op jit(solution)/shard_map/ppermute | solution.py:371
  5.6 1.3 %collective-permute-start.1 = (f32[2,3,8,1024]{3,2,1,0:T(8,128)S(1)}, f32[2,3,8,1024]{3,2,1,0:T(8,128)S(1)}, u32[]{:S(2)}, u32[]{:S(2)}) collective-permute-start(f32[2,3,8,1024]{3,2,1,0:T(8,128)S(1)} %get-tuple-element.12), channel_id=1, source_target_pairs={{1,0},{2,1},{3,2},{4,3},{5,4},{6,5},{7,6},{8,7},{9,8},{10,9},{11,1... | collective-permute-start | bytes 589832 | tf_op jit(solution)/shard_map/ppermute | solution.py:372
  6.9 0.0 copy-done
  6.9 0.0 copy-done.2
  6.9 0.0 copy-start.1
  6.9 0.9 %copy-done.1 = s32[32,1024]{1,0:T(8,128)S(1)} copy-done((s32[32,1024]{1,0:T(8,128)S(1)}, s32[32,1024]{1,0:T(8,128)}, u32[]{:S(2)}) %copy-start.1) | copy-done | bytes 131096
  7.8 3.9 %vorticity_inside.1 = (f32[8,32,8,128]{3,2,1,0:T(8,128)S(1)}, f32[2,32,1024]{2,1,0:T(8,128)S(1)}) custom-call(f32[4,16]{1,0:T(4,128)S(1)} %copy-done.2, f32[2,256,1024]{2,1,0:T(8,128)S(1)} %bitcast.2, s32[32,1024]{1,0:T(8,128)S(1)} %copy-done.1), custom_call_target="tpu_custom_call" | custom-call | flops 4000000000 | bytes 4194304 | tf_op jit(solution)/shard_map/vorticity_inside/pallas_call | solution.py:135
  11.7 0.0 collective-permute-done.before
  11.7 2.1 %collective-permute-done.1.after = f32[2,3,8,1024]{3,2,1,0:T(8,128)S(1)} collective-permute-done((f32[2,3,8,1024]{3,2,1,0:T(8,128)S(1)}, f32[2,3,8,1024]{3,2,1,0:T(8,128)S(1)}, u32[]{:S(2)}, u32[]{:S(2)}) %collective-permute-start.1) | collective-permute-done | bytes 196640 | tf_op jit(solution)/shard_map/ppermute | solution.py:372
  13.8 0.1 border.1
  13.9 20.1 %all_to_all.20.z_ref = f32[8,32,8,128]{3,2,1,0:T(8,128)S(1)} all-to-all(f32[8,32,8,128]{3,2,1,0:T(8,128)S(1)} %border.1), channel_id=1, replica_groups=mesh['snap'=8,'space'=64] {'snap'}, dimensions={0} | all-to-all | bytes 2097152 | tf_op jit(solution)/shard_map/all_to_all | solution.py:376
  34.0 0.8 gram.1
  34.8 8.2 %all_to_all.21.in_ref = f32[8,24,128]{2,1,0:T(8,128)S(1)} all-to-all(f32[8,24,128]{2,1,0:T(8,128)S(1)} %get-tuple-element.14), channel_id=1, replica_groups=mesh['snap'=8,'space'=64] {'snap'}, dimensions={0} | all-to-all | bytes 196608 | tf_op jit(solution)/shard_map/all_to_all | solution.py:384
  43.0 15.0 %all_to_all.22.in_ref = f32[8,24,128]{2,1,0:T(8,128)S(1)} all-to-all(f32[8,24,128]{2,1,0:T(8,128)S(1)} %summed.2), channel_id=1, replica_groups={{0,1,2,3,4,5,6,7},{8,9,10,11,12,13,14,15},{16,17,18,19,20,21,22,23},{24..., dimensions={0} | all-to-all | bytes 196608 | tf_op jit(solution)/shard_map/all_to_all | solution.py:384
  58.0 18.8 %all_to_all.23.sum_ref = f32[8,24,128]{2,1,0:T(8,128)S(1)} all-to-all(f32[8,24,128]{2,1,0:T(8,128)S(1)} %summed.3), channel_id=1, replica_groups={{0,8,16,24,32,40,48,56},{1,9,17,25,33,41,49,57},{2,10,18,26,34,42,50,58..., dimensions={0} | all-to-all | bytes 196608 | tf_op jit(solution)/shard_map/all_to_all | solution.py:384
  76.9 3.8 %modes.1 = (f32[2016,128]{1,0:T(8,128)}, f32[63,63]{1,0:T(8,128)}) custom-call(f32[8,24,128]{2,1,0:T(8,128)S(1)} %all_to_all.23.sum_ref, bf16[192,4096]{1,0:T(8,128)(2,1)S(1)} %get-tuple-element.15.parts_ref), custom_call_target="tpu_custom_call" | custom-call | tf_op jit(solution)/shard_map/modes/pallas_call | solution.py:343
  (2 shorter events, 0.0 us)
Async XLA Ops:
  0.6 6.2 %copy-start = (f32[2,8,32,1024]{3,2,1,0:T(8,128)S(1)}, f32[2,8,32,1024]{3,2,1,0:T(8,128)}, u32[]{:S(2)}) copy-start(f32[2,8,32,1024]{3,2,1,0:T(8,128)} %vel.1) | copy-start | bytes 6291460
  0.6 6.2 %copy-start.2 = (f32[4,16]{1,0:T(4,128)S(1)}, f32[4,16]{1,0:T(4,128)}, u32[]{:S(2)}) copy-start(f32[4,16]{1,0:T(4,128)} %table.1) | copy-start | bytes 772
  2.1 9.7 %collective-permute-start = (f32[2,3,8,1024]{3,2,1,0:T(8,128)S(1)}, f32[2,3,8,1024]{3,2,1,0:T(8,128)S(1)}, u32[]{:S(2)}, u32[]{:S(2)}) collective-permute-start(f32[2,3,8,1024]{3,2,1,0:T(8,128)S(1)} %get-tuple-element.11), channel_id=1, source_target_pairs={{0,1},{1,2},{2,3},{3,4},{4,5},{5,6},{6,7},{7,8},{8,9},{9,10},{10,1... | collective-permute-start | bytes 589832 | tf_op jit(solution)/shard_map/ppermute | solution.py:371
  5.6 8.3 %collective-permute-start.1 = (f32[2,3,8,1024]{3,2,1,0:T(8,128)S(1)}, f32[2,3,8,1024]{3,2,1,0:T(8,128)S(1)}, u32[]{:S(2)}, u32[]{:S(2)}) collective-permute-start(f32[2,3,8,1024]{3,2,1,0:T(8,128)S(1)} %get-tuple-element.12), channel_id=1, source_target_pairs={{1,0},{2,1},{3,2},{4,3},{5,4},{6,5},{7,6},{8,7},{9,8},{10,9},{11,1... | collective-permute-start | bytes 589832 | tf_op jit(solution)/shard_map/ppermute | solution.py:372
  6.9 0.9 %copy-start.1 = (s32[32,1024]{1,0:T(8,128)S(1)}, s32[32,1024]{1,0:T(8,128)}, u32[]{:S(2)}) copy-start(s32[32,1024]{1,0:T(8,128)} %index_ref.1) | copy-start | bytes 393220

commit v6 on v5

--- a/solution.py
+++ b/solution.py
@@ -100,9 +100,8 @@
             out_ref[p, out_first + s] = total
 
 
-def vorticity_kernel(table, vel, index_ref, out_ref, edge_ref, lines):
-    rows, cols = index_ref.shape
-    snaps, blocks = vel.shape[1] // rows, cols // 128
+def turn_kernel(rows, vel, lines):
+    snaps, blocks = vel.shape[1] // rows, vel.shape[2] // 128
     zero = jnp.zeros((2, blocks, 3 * snaps, 128), F32)
     lines[:, :, : 3 * snaps] = zero
     lines[:, :, (rows + 3) * snaps :] = zero
@@ -113,6 +112,11 @@
                     tile = vel[c, m * rows + r : m * rows + r + 8, 128 * p : 128 * p + 128]
                     lines[c, p, pl.ds((r + 3) * snaps + m, 8, stride=snaps), :] = tile
 
+
+def vorticity_kernel(table, lines, index_ref, out_ref, edge_ref):
+    rows, cols = index_ref.shape
+    snaps, blocks = lines.shape[2] // (rows + 6), cols // 128
+
     def band(r, carry):
         top = 8 * r
 
@@ -132,6 +136,15 @@
 def vorticity_inside(table, flat, index):
     rows, cols = index.shape
     snaps, blocks = flat.shape[1] // rows, cols // 128
+    lines = pl.pallas_call(
+        functools.partial(turn_kernel, rows),
+        out_shape=jax.ShapeDtypeStruct((2, blocks, (rows + 6) * snaps, 128), F32),
+        in_specs=[VMEM],
+        out_specs=VMEM,
+        compiler_params=params(16),
+        cost_estimate=cost(500000000, MIB),
+        name="turn",
+    )(flat)
     return pl.pallas_call(
         vorticity_kernel,
         out_shape=(
@@ -140,11 +153,10 @@
         ),
         in_specs=[SMEM, VMEM, VMEM],
         out_specs=(VMEM, VMEM),
-        scratch_shapes=[pltpu.VMEM((2, blocks, (rows + 6) * snaps, 128), F32)],
         compiler_params=params(16),
         cost_estimate=cost(4000000000, 4 * MIB),
         name="vorticity_inside",
-    )(table, flat, index)
+    )(table, lines, index)
 
 
 def border_kernel(part_ref, before, after, edge, out_ref):

time: 81 us -> 81 us (level)
  transfers between devices with their start and end apart: 2 -> 2, of which waited for: 1 -> 1; matrix products, arithmetic and copies ran while one was open for 0% -> 0% of each run, Pallas kernels for 5% -> 6%
where the time goes in v6:
time: 81 us; the launch traced here: 80.7 us
  blocking collectives  62.1 us (77%)
  Pallas kernels  10.6 us (13%)
  starting transfers between devices  4.78 us (6%)
  waiting for transfers between devices  2.15 us (3%)
    all_to_all x3, blocking collectives, local(): arrived = lax.all_to_all(sent, axis, 0, 0, axis_index_groups=groups)  42 us
    all_to_all x1, blocking collectives, local(): owned = lax.all_to_all(whole, 'snap', 0, 0)  20.1 us
    pallas_call x1, Pallas kernels, vorticity_inside(): pl.pallas_call(vorticity_kernel, out_shape=(jax.ShapeDtypeStruct((blocks,...  3.87 us
    pallas_call x1, Pallas kernels, modes_of(): pl.pallas_call(modes_kernel, out_shape=(jax.ShapeDtypeStruct(((snaps - 1)...  3.84 us
    ppermute x1, starting transfers between devices, local(): before = lax.ppermute(last, 'space', up)  3.49 us
    ppermute x1, waiting for transfers between devices, local(): after = lax.ppermute(first, 'space', down)  2.15 us
  transfers between devices with their start and end apart: 2, of which 1 were waited for; matrix products, arithmetic and copies ran while one was open for 0% of the time, Pallas kernels for 6%

profile of v6, /device:TPU:2, one launch (start us, length us, event | category | flops | bytes accessed | tf_op | source)
XLA Modules:
  0.0 80.7 jit_solution(704523746177042662)
XLA Ops:
  0.6 0.0 copy-start
  0.6 1.4 %edges.1 = (f32[2,3,8,1024]{3,2,1,0:T(8,128)S(1)}, f32[2,3,8,1024]{3,2,1,0:T(8,128)S(1)}) custom-call(f32[2,8,32,1024]{3,2,1,0:T(8,128)} %vel.1), custom_call_target="tpu_custom_call" | custom-call | tf_op jit(solution)/shard_map/edges/pallas_call | solution.py:47
  2.0 3.5 %collective-permute-start = (f32[2,3,8,1024]{3,2,1,0:T(8,128)S(1)}, f32[2,3,8,1024]{3,2,1,0:T(8,128)S(1)}, u32[]{:S(2)}, u32[]{:S(2)}) collective-permute-start(f32[2,3,8,1024]{3,2,1,0:T(8,128)S(1)} %get-tuple-element.11), channel_id=1, source_target_pairs={{0,1},{1,2},{2,3},{3,4},{4,5},{5,6},{6,7},{7,8},{8,9},{9,10},{10,1... | collective-permute-start | bytes 589832 | tf_op jit(solution)/shard_map/ppermute | solution.py:383
  5.5 1.3 %collective-permute-start.1 = (f32[2,3,8,1024]{3,2,1,0:T(8,128)S(1)}, f32[2,3,8,1024]{3,2,1,0:T(8,128)S(1)}, u32[]{:S(2)}, u32[]{:S(2)}) collective-permute-start(f32[2,3,8,1024]{3,2,1,0:T(8,128)S(1)} %get-tuple-element.12), channel_id=1, source_target_pairs={{1,0},{2,1},{3,2},{4,3},{5,4},{6,5},{7,6},{8,7},{9,8},{10,9},{11,1... | collective-permute-start | bytes 589832 | tf_op jit(solution)/shard_map/ppermute | solution.py:384
  6.8 0.0 copy-done
  6.9 0.0 copy-start.1
  6.9 0.0 copy-start.2
  6.9 0.6 turn.1.lines
  7.5 0.3 copy-done.1
  7.8 0.0 copy-done.2
  7.8 3.9 %vorticity_inside.1 = (f32[8,32,8,128]{3,2,1,0:T(8,128)S(1)}, f32[2,32,1024]{2,1,0:T(8,128)S(1)}) custom-call(f32[4,16]{1,0:T(4,128)S(1)} %copy-done.2, f32[2,8,304,128]{3,2,1,0:T(8,128)S(1)} %turn.1.lines, s32[32,1024]{1,0:T(8,128)S(1)} %copy-done.1), custom_call_target="tpu_custom_call" | custom-call | flops 4000000000 | bytes 4194304 | tf_op jit(solution)/shard_map/vorticity_inside/pallas_call | solution.py:148
  11.6 0.0 collective-permute-done.before
  11.7 2.1 %collective-permute-done.1.after = f32[2,3,8,1024]{3,2,1,0:T(8,128)S(1)} collective-permute-done((f32[2,3,8,1024]{3,2,1,0:T(8,128)S(1)}, f32[2,3,8,1024]{3,2,1,0:T(8,128)S(1)}, u32[]{:S(2)}, u32[]{:S(2)}) %collective-permute-start.1) | collective-permute-done | bytes 196640 | tf_op jit(solution)/shard_map/ppermute | solution.py:384
  13.8 0.1 border.1
  13.9 20.1 %all_to_all.20.z_ref = f32[8,32,8,128]{3,2,1,0:T(8,128)S(1)} all-to-all(f32[8,32,8,128]{3,2,1,0:T(8,128)S(1)} %border.1), channel_id=1, replica_groups=mesh['snap'=8,'space'=64] {'snap'}, dimensions={0} | all-to-all | bytes 2097152 | tf_op jit(solution)/shard_map/all_to_all | solution.py:388
  34.0 0.8 gram.1
  34.8 8.2 %all_to_all.21.in_ref = f32[8,24,128]{2,1,0:T(8,128)S(1)} all-to-all(f32[8,24,128]{2,1,0:T(8,128)S(1)} %get-tuple-element.14), channel_id=1, replica_groups=mesh['snap'=8,'space'=64] {'snap'}, dimensions={0} | all-to-all | bytes 196608 | tf_op jit(solution)/shard_map/all_to_all | solution.py:396
  43.0 15.0 %all_to_all.22.in_ref = f32[8,24,128]{2,1,0:T(8,128)S(1)} all-to-all(f32[8,24,128]{2,1,0:T(8,128)S(1)} %summed.2), channel_id=1, replica_groups={{0,1,2,3,4,5,6,7},{8,9,10,11,12,13,14,15},{16,17,18,19,20,21,22,23},{24..., dimensions={0} | all-to-all | bytes 196608 | tf_op jit(solution)/shard_map/all_to_all | solution.py:396
  58.0 18.8 %all_to_all.23.sum_ref = f32[8,24,128]{2,1,0:T(8,128)S(1)} all-to-all(f32[8,24,128]{2,1,0:T(8,128)S(1)} %summed.3), channel_id=1, replica_groups={{0,8,16,24,32,40,48,56},{1,9,17,25,33,41,49,57},{2,10,18,26,34,42,50,58..., dimensions={0} | all-to-all | bytes 196608 | tf_op jit(solution)/shard_map/all_to_all | solution.py:396
  76.9 3.8 %modes.1 = (f32[2016,128]{1,0:T(8,128)}, f32[63,63]{1,0:T(8,128)}) custom-call(f32[8,24,128]{2,1,0:T(8,128)S(1)} %all_to_all.23.sum_ref, bf16[192,4096]{1,0:T(8,128)(2,1)S(1)} %get-tuple-element.15.parts_ref), custom_call_target="tpu_custom_call" | custom-call | tf_op jit(solution)/shard_map/modes/pallas_call | solution.py:355
  (2 shorter events, 0.0 us)
Async XLA Ops:
  0.6 6.2 %copy-start = (f32[2,8,32,1024]{3,2,1,0:T(8,128)S(1)}, f32[2,8,32,1024]{3,2,1,0:T(8,128)}, u32[]{:S(2)}) copy-start(f32[2,8,32,1024]{3,2,1,0:T(8,128)} %vel.1) | copy-start | bytes 6291460
  2.0 9.6 %collective-permute-start = (f32[2,3,8,1024]{3,2,1,0:T(8,128)S(1)}, f32[2,3,8,1024]{3,2,1,0:T(8,128)S(1)}, u32[]{:S(2)}, u32[]{:S(2)}) collective-permute-start(f32[2,3,8,1024]{3,2,1,0:T(8,128)S(1)} %get-tuple-element.11), channel_id=1, source_target_pairs={{0,1},{1,2},{2,3},{3,4},{4,5},{5,6},{6,7},{7,8},{8,9},{9,10},{10,1... | collective-permute-start | bytes 589832 | tf_op jit(solution)/shard_map/ppermute | solution.py:383
  5.5 8.3 %collective-permute-start.1 = (f32[2,3,8,1024]{3,2,1,0:T(8,128)S(1)}, f32[2,3,8,1024]{3,2,1,0:T(8,128)S(1)}, u32[]{:S(2)}, u32[]{:S(2)}) collective-permute-start(f32[2,3,8,1024]{3,2,1,0:T(8,128)S(1)} %get-tuple-element.12), channel_id=1, source_target_pairs={{1,0},{2,1},{3,2},{4,3},{5,4},{6,5},{7,6},{8,7},{9,8},{10,9},{11,1... | collective-permute-start | bytes 589832 | tf_op jit(solution)/shard_map/ppermute | solution.py:384
  6.9 0.9 %copy-start.1 = (s32[32,1024]{1,0:T(8,128)S(1)}, s32[32,1024]{1,0:T(8,128)}, u32[]{:S(2)}) copy-start(s32[32,1024]{1,0:T(8,128)} %index_ref.1) | copy-start | bytes 393220
  6.9 0.9 %copy-start.2 = (f32[4,16]{1,0:T(4,128)S(1)}, f32[4,16]{1,0:T(4,128)}, u32[]{:S(2)}) copy-start(f32[4,16]{1,0:T(4,128)} %table.1) | copy-start | bytes 772
